TPU v7x, 512 devices: a whole 4x4x16 slice. The times are simulated.
512 devices in a mesh: row: 16 (over z_lo, core), col: 32 (over y, z_hi, x).
Axes of the slice: x: 4, y: 4, z: 16 (z_hi: 2, z_lo: 8; z = z_hi * 8 + z_lo), core: 2. Of those that a mesh axis runs over, the one named last changes fastest.
Arguments:
- field_rhs: float32 [16, 32, 2, 3, 512], P('row', 'col'), may hold values from -6 to 6
- positions: float32 [16, 32, 3, 512], P('row', 'col'), may hold values from 0.25 to 255.75, as said below
- polar: float32 [16, 32, 512], P('row', 'col'), may hold values from 0.5 to 4
- grid_base: int32 [16, 32, 3, 512], P('row', 'col'), may hold values from 0 to 255, as said below
- tile_lists: int32 [16, 32, 4, 12], P('row', 'col'), may hold values from 0 to 35, as said below
Outputs:
- dipoles: float32 [16, 32, 2, 3, 512], P('row', 'col')
- residual: float32 [16, 32, 2, 3, 512], P('row', 'col')
Inputs may be any that keep to these rules, and one draw needn't show every extreme that they name: grid_base + 2, modulo the grid's length in that dimension, is the grid cell holding the atom; the atoms of brick (r, c) lie in its cells r * 8 to r * 8 + 7 along x and c * 4 to c * 4 + 3 along y, no two atoms share a cell, and atom t * 128 + i of a brick lies in z cells t * 64 to (t + 1) * 64 - 1. positions minus the atom's cell lies in 0.25 to 0.75 in every dimension. `tile_lists`: entry k of tile t names a tile of the 3 x 3 bricks around the tile's own brick as value = b * 4 + tile with brick offset (b // 3 - 1, b mod 3 - 1); entry 0 is tile t itself (b = 4); the entries of one list are distinct, and each other entry is tile t - 1, t or t + 1 (modulo 4) of its brick.
All inputs are finite; a program needn't handle non-finite values.
Results may differ from a plain program's by a relative error of at most 0.0003.
Values sent between devices are 32-bit elements; how exact they have to be, the bound alone decides.
A program may use at most 64 MiB of HBM per device.

v0:
```python
import math

import jax
import jax.numpy as jnp
from jax import lax
from jax.sharding import PartitionSpec as P

CX = 8
CY = 4
KZ = 256
TILE = 128
RHS = 2
ITERS = 2


ewald_beta = 0.4
thole_a = 0.39
self_coef = 4.0 * ewald_beta**3 / (3.0 * math.sqrt(math.pi))
highest = lax.Precision.HIGHEST


def with_halo(cells, sides, width):
    for axis, dim in sides:
        count = lax.axis_size(axis)
        head = lax.slice_in_dim(cells, 0, width, axis=dim)
        tail = lax.slice_in_dim(cells, cells.shape[dim] - width, cells.shape[dim], axis=dim)
        cells = jnp.concatenate(
            [
                lax.ppermute(tail, axis, [(i, (i + 1) % count) for i in range(count)]),
                cells,
                lax.ppermute(head, axis, [((i + 1) % count, i) for i in range(count)]),
            ],
            axis=dim,
        )
    return cells


def spline_table(fraction):
    previous = {0: jnp.ones_like(fraction)}
    fourth = previous
    for degree in range(2, 6):
        current = {}
        for offset in range(degree):
            abscissa = fraction + offset
            summed = abscissa * previous.get(offset, 0.0) + (degree - abscissa) * previous.get(
                offset - 1, 0.0
            )
            current[offset] = summed / (degree - 1)
        if degree == 4:
            fourth = current
        previous = current
    values = jnp.stack([previous[4 - stencil] for stencil in range(5)])
    slopes = jnp.stack(
        [fourth.get(4 - stencil, 0.0) - fourth.get(3 - stencil, 0.0) for stencil in range(5)]
    )
    return (values, slopes)


def spline_modulus(wave_index, length):
    spline_coef = (1.0 / 24.0, 11.0 / 24.0, 11.0 / 24.0, 1.0 / 24.0)
    cosine_sum = jnp.zeros(wave_index.shape, jnp.float32)
    sine_sum = jnp.zeros(wave_index.shape, jnp.float32)
    for offset in range(4):
        angles = 2.0 * math.pi / length * (wave_index * offset % length).astype(jnp.float32)
        cosine_sum = cosine_sum + spline_coef[offset] * jnp.cos(angles)
        sine_sum = sine_sum + spline_coef[offset] * jnp.sin(angles)
    return cosine_sum * cosine_sum + sine_sum * sine_sum


def folded_square(wave_index, length):
    nearest = jnp.minimum(wave_index, length - wave_index).astype(jnp.float32) / length
    return nearest * nearest


def influence(wave_x, wave_y, wave_z, length_x, length_y, length_z):
    wave_norm = (
        folded_square(wave_x, length_x)
        + folded_square(wave_y, length_y)
        + folded_square(wave_z, length_z)
    )
    modulus = (
        spline_modulus(wave_x, length_x)
        * spline_modulus(wave_y, length_y)
        * spline_modulus(wave_z, length_z)
    )
    excluded = (wave_x * 2 == length_x) | (wave_y * 2 == length_y) | (wave_z * 2 == length_z)
    excluded = excluded | (wave_x == 0) & (wave_y == 0) & (wave_z == 0)
    safe_norm = jnp.where(excluded, 1.0, wave_norm)
    safe_modulus = jnp.where(excluded, 1.0, modulus)
    result = jnp.exp(-(math.pi**2 / ewald_beta**2) * safe_norm) / (
        math.pi * safe_norm * safe_modulus
    )
    return jnp.where(excluded, 0.0, result)


def tile_field(own_static, near_static, near_dipole, box_spans):
    listed_count = near_static.shape[0]
    tile_width = own_static.shape[1]
    box_span = jnp.array(box_spans, dtype=jnp.float32)[None, :, None, None]
    separation = near_static[:, 0:3, None, :] - own_static[None, 0:3, :, None]
    separation = separation - box_span * jnp.floor(separation / box_span + 0.5)
    dist_sq = jnp.sum(separation * separation, axis=1)
    itself = (jnp.arange(listed_count)[:, None, None] == 0) & (
        jnp.arange(tile_width)[:, None] == jnp.arange(tile_width)[None, :]
    )[None]
    safe_sq = jnp.where(itself, 1.0, dist_sq)
    distance = jnp.sqrt(safe_sq)
    scaled = distance / (own_static[3][None, :, None] * near_static[:, 3][:, None, :])
    cubed = thole_a * scaled * scaled * scaled
    damping = jnp.exp(-cubed)
    screen = lax.erfc(ewald_beta * distance)
    gaussian = 2.0 * ewald_beta / math.sqrt(math.pi) * jnp.exp(-(ewald_beta * ewald_beta) * safe_sq)
    inverse_sq = 1.0 / safe_sq
    inverse_cube = inverse_sq / distance
    first_term = (screen - damping) * inverse_cube + gaussian * inverse_sq
    second = (
        3.0 * (screen - (1.0 + cubed) * damping) * inverse_cube * inverse_sq
        + gaussian * (2.0 * ewald_beta * ewald_beta + 3.0 * inverse_sq) * inverse_sq
    )
    first_term = jnp.where(itself, 0.0, first_term)
    second = jnp.where(itself, 0.0, second)
    projected = jnp.sum(near_dipole[:, :, :, None, :] * separation[:, None, :, :, :], axis=2)
    weighted = second[:, None] * projected
    outward = jnp.sum(weighted[:, :, None] * separation[:, None], axis=(0, 4))
    inward = jnp.sum(first_term[:, None, None] * near_dipole[:, :, :, None, :], axis=(0, 4))
    return outward - inward


def hartley(length):
    counter = jnp.arange(length, dtype=jnp.int32)
    angles = (
        2.0 * math.pi / length * (counter[:, None] * counter[None, :] % length).astype(jnp.float32)
    )
    return jnp.cos(angles) + jnp.sin(angles)


def placed_table(first_cell, weights, extent):
    slot_index = jnp.arange(extent, dtype=jnp.int32)[:, None]
    placed = jnp.zeros((extent, first_cell.shape[0]), jnp.float32)
    for stencil in range(5):
        placed = placed + jnp.where(
            slot_index == (first_cell[None, :] + stencil) % extent, weights[stencil][None, :], 0.0
        )
    return placed


def pad_axis(source, axis_pos, leading, trailing):
    widths = [(0, 0)] * source.ndim
    widths[axis_pos] = (leading, trailing)
    return jnp.pad(source, widths)


def fold_cycle(cycle_only, axis_pos, inner_len):
    middle = lax.slice_in_dim(cycle_only, 4, inner_len + 4, axis=axis_pos)
    lower_cycle = lax.slice_in_dim(cycle_only, 0, 2, axis=axis_pos)
    upper_cycle = lax.slice_in_dim(cycle_only, inner_len + 6, inner_len + 8, axis=axis_pos)
    return (
        middle
        + pad_axis(lower_cycle, axis_pos, 0, inner_len - 2)
        + pad_axis(upper_cycle, axis_pos, inner_len - 2, 0)
    )


def clear_inside(extended, extents):
    inside = None
    for axis_pos, inner_len in extents:
        slot_index = lax.broadcasted_iota(jnp.int32, extended.shape, axis_pos)
        within = (slot_index >= 2) & (slot_index < inner_len + 6)
        inside = within if inside is None else inside & within
    return jnp.where(inside, 0.0, extended)


def inner_sum(left_arr, right_arr):
    return lax.psum(jnp.sum(left_arr * right_arr, axis=(1, 2)), ("row", "col"))


def local(field_rhs, positions, polar, grid_base, tile_lists):
    rows_count = lax.axis_size("row")
    cols_count = lax.axis_size("col")
    grid_x = CX * rows_count
    grid_y = CY * cols_count
    atom_count = polar.shape[-1]
    tile_count = atom_count // TILE
    slab_depth = KZ // tile_count
    window_len = slab_depth + 4
    box_spans = (float(grid_x), float(grid_y), float(KZ))
    own_place = positions[0, 0]
    own_base = grid_base[0, 0]
    own_polar = polar[0, 0]
    lengths = jnp.array([grid_x, grid_y, KZ], dtype=jnp.int32)[:, None]
    cell_index = (own_base + 2) % lengths
    fraction = own_place - cell_index.astype(jnp.float32)
    values, slopes = spline_table(fraction)
    first_x = (own_base[0] - lax.axis_index("row") * CX + 2) % grid_x
    first_y = (own_base[1] - lax.axis_index("col") * CY + 2) % grid_y
    rows_x = placed_table(first_x, values[:, 0], CX + 4)
    slope_x = placed_table(first_x, slopes[:, 0], CX + 4)
    rows_y = placed_table(first_y, values[:, 1], CY + 4)
    slope_y = placed_table(first_y, slopes[:, 1], CY + 4)
    tile_start = jnp.arange(atom_count, dtype=jnp.int32) // TILE * slab_depth
    first_z = (own_base[2] + 2 - tile_start) % KZ
    rows_z = placed_table(first_z, values[:, 2], window_len)
    slope_z = placed_table(first_z, slopes[:, 2], window_len)
    plane_count = (CX + 4) * (CY + 4)
    plane_dx = (slope_x[:, None, :] * rows_y[None, :, :]).reshape(plane_count, atom_count)
    plane_dy = (rows_x[:, None, :] * slope_y[None, :, :]).reshape(plane_count, atom_count)
    plane_flat = (rows_x[:, None, :] * rows_y[None, :, :]).reshape(plane_count, atom_count)
    window_rows = jnp.moveaxis(rows_z.reshape(window_len, tile_count, TILE), 1, 0)
    window_slope = jnp.moveaxis(slope_z.reshape(window_len, tile_count, TILE), 1, 0)
    depth_table = jnp.concatenate([window_rows, window_slope], axis=2)
    grid_scale = 1.0 / (grid_x * grid_y * KZ)
    hartley_x = hartley(grid_x)
    hartley_y = hartley(grid_y)
    hartley_z = hartley(KZ)
    block_y = grid_y // rows_count
    block_z = KZ // cols_count
    wave_x = jnp.arange(grid_x, dtype=jnp.int32)[:, None, None]
    wave_y = (lax.axis_index("row") * block_y + jnp.arange(block_y, dtype=jnp.int32))[None, :, None]
    wave_z = (lax.axis_index("col") * block_z + jnp.arange(block_z, dtype=jnp.int32))[None, None, :]
    kernel = influence(wave_x, wave_y, wave_z, grid_x, grid_y, KZ) * grid_scale
    root_scale = jnp.power(own_polar, 1.0 / 6.0)
    own_static = jnp.concatenate([own_place, root_scale[None]], axis=0)
    near_static = with_halo(own_static[None, None], (("row", 0), ("col", 1)), 1)
    near_static = jnp.moveaxis(near_static.reshape(9, 4, tile_count, TILE), 2, 1).reshape(
        9 * tile_count, 4, TILE
    )
    own_tiles = jnp.moveaxis(own_static.reshape(4, tile_count, TILE), 1, 0)
    own_lists = tile_lists[0, 0]
    polar_wide = own_polar[None, None, :]
    solution = jnp.zeros_like(field_rhs[0, 0])
    residual = field_rhs[0, 0]
    scaled_res = polar_wide * residual
    direction = scaled_res
    progress = inner_sum(residual, scaled_res)
    for iteration in range(ITERS):
        near_dip = with_halo(direction[None, None], (("row", 0), ("col", 1)), 1)
        near_dip = jnp.moveaxis(near_dip.reshape(9, RHS, 3, tile_count, TILE), 3, 1).reshape(
            9 * tile_count, RHS, 3, TILE
        )

        def one_tile(tile_pos):
            picked = own_lists[tile_pos]
            return tile_field(own_tiles[tile_pos], near_static[picked], near_dip[picked], box_spans)

        fields = lax.map(one_tile, jnp.arange(tile_count, dtype=jnp.int32))
        direct = jnp.moveaxis(fields, 0, 2).reshape(RHS, 3, atom_count)
        slope_terms = (
            direction[:, 0, None, :] * plane_dx[None] + direction[:, 1, None, :] * plane_dy[None]
        )
        flat_terms = direction[:, 2, None, :] * plane_flat[None]
        spread_left = jnp.concatenate(
            [
                slope_terms.reshape(RHS, plane_count, tile_count, TILE),
                flat_terms.reshape(RHS, plane_count, tile_count, TILE),
            ],
            axis=3,
        )
        spread_windows = jnp.einsum("sptb,twb->sptw", spread_left, depth_table, precision=highest)
        main_part = spread_windows[..., :slab_depth].reshape(spread_windows.shape[:-2] + (KZ,))
        tail_part = pad_axis(
            spread_windows[..., slab_depth:], spread_windows.ndim - 1, 0, slab_depth - 4
        )
        tail_part = tail_part.reshape(spread_windows.shape[:-2] + (KZ,))[..., : KZ + 4 - slab_depth]
        last_axis = main_part.ndim - 1
        padded_line = pad_axis(main_part, last_axis, 0, 4) + pad_axis(
            tail_part, last_axis, slab_depth, 0
        )
        inner = padded_line[..., 2 : KZ + 2]
        spread_tile = (
            inner
            + pad_axis(padded_line[..., 0:2], last_axis, KZ - 2, 0)
            + pad_axis(padded_line[..., KZ + 2 : KZ + 4], last_axis, 0, KZ - 2)
        ).reshape(RHS, CX + 4, CY + 4, KZ)
        extended = with_halo(spread_tile, (("row", 1), ("col", 2)), 2)
        cycle_only = clear_inside(extended, ((1, CX), (2, CY)))
        folded = fold_cycle(fold_cycle(cycle_only, 1, CX), 2, CY)
        spectrum = jnp.einsum(
            "sxyz,zk->sxyk",
            spread_tile[:, 2 : CX + 2, 2 : CY + 2] + folded,
            hartley_z,
            precision=highest,
        )
        along_y = jnp.einsum(
            "sxyz,yk->sxkz",
            lax.all_to_all(spectrum, "col", split_axis=3, concat_axis=2, tiled=True),
            hartley_y,
            precision=highest,
        )
        along_x = (
            jnp.einsum(
                "sxyz,xk->skyz",
                lax.all_to_all(along_y, "row", split_axis=2, concat_axis=1, tiled=True),
                hartley_x,
                precision=highest,
            )
            * kernel[None]
        )
        mixed_part = jnp.einsum("sxyz,xk->skyz", along_x, hartley_x, precision=highest)
        returned = lax.all_to_all(mixed_part, "row", split_axis=1, concat_axis=2, tiled=True)
        swapped = jnp.einsum("sxyz,yk->sxkz", returned, hartley_y, precision=highest)
        restored = lax.all_to_all(swapped, "col", split_axis=2, concat_axis=3, tiled=True)
        padded = with_halo(
            jnp.einsum("sxyz,zk->sxyk", restored, hartley_z, precision=highest),
            (("row", 1), ("col", 2)),
            2,
        )
        line = padded.reshape(RHS, plane_count, KZ)
        extended_line = jnp.concatenate([line[..., KZ - 2 :], line, line[..., :2]], axis=-1)
        windows = jnp.stack(
            [
                extended_line[..., tile * slab_depth : tile * slab_depth + window_len]
                for tile in range(tile_count)
            ],
            axis=-2,
        )
        sampled = jnp.einsum("sptw,twb->sptb", windows, depth_table, precision=highest)
        with_flat = sampled[..., :TILE].reshape(RHS, plane_count, atom_count)
        with_slope = sampled[..., TILE:].reshape(RHS, plane_count, atom_count)
        recip_part = jnp.stack(
            [
                jnp.sum(with_flat * plane_dx[None], axis=1),
                jnp.sum(with_flat * plane_dy[None], axis=1),
                jnp.sum(with_slope * plane_flat[None], axis=1),
            ],
            axis=1,
        )
        image_field = direction / polar_wide - direct + recip_part - self_coef * direction
        step_size = (progress / inner_sum(direction, image_field))[:, None, None]
        solution = solution + step_size * direction
        residual = residual - step_size * image_field
        scaled_res = polar_wide * residual
        progress_next = inner_sum(residual, scaled_res)
        direction = scaled_res + (progress_next / progress)[:, None, None] * direction
        progress = progress_next
    return (solution[None, None], residual[None, None])


def solution(mesh):
    placed = (
        P("row", "col", None, None, None),
        P("row", "col", None, None),
        P("row", "col", None),
        P("row", "col", None, None),
        P("row", "col", None, None),
    )
    return jax.shard_map(
        local,
        mesh=mesh,
        in_specs=placed,
        out_specs=(P("row", "col", None, None, None), P("row", "col", None, None, None)),
        check_vma=False,
    )
```

profile of v0, /device:TPU:1, one launch (start us, length us, event | category | flops | bytes accessed | tf_op | source)
XLA Modules:
  0.0 879.4 jit_solution(1946243871823307928)
XLA Ops:
  2.0 8.8 collective-permute-start.1
  18.1 7.2 collective-permute-start.9
  27.8 8.5 collective-permute-done.8
  36.3 12.6 %collective-permute-start.11 = (f32[2,16,2,256]{3,2,1,0:T(2,128)S(1)}, f32[2,16,2,256]{3,2,1,0:T(2,128)S(1)}, u32[]{:S(2)}, u32[]{:S(2)}) collective-permute-start(f32[2,16,2,256]{3,2,1,0:T(2,128)S(1)} %get-tuple-element.269), channel_id=1, source_target_pairs={{1,0},{2,1},{3,2},{4,3},{5,4},{6,5},{7,6},{8,7},{9,8},{10,9},{11,1... | collective-permute-start | bytes 196616 | tf_op jit(solution)/shard_map/ppermute | solution.py:31
  50.9 16.0 %collective-permute-done.10 = f32[2,16,2,256]{3,2,1,0:T(2,128)S(1)} collective-permute-done((f32[2,16,2,256]{3,2,1,0:T(2,128)S(1)}, f32[2,16,2,256]{3,2,1,0:T(2,128)S(1)}, u32[]{:S(2)}, u32[]{:S(2)}) %collective-permute-start.10) | collective-permute-done | bytes 65568 | tf_op jit(solution)/shard_map/ppermute | solution.py:29
  74.9 16.0 %all-to-all-done = f32[32,1,512]{2,1,0:T(1,128)S(1)} async-done(((f32[32,1,512]{2,1,0:T(1,128)}), f32[32,1,512]{2,1,0:T(1,128)S(1)}, u32[]{:S(2)}, u32[]{:S(2)}) %all-to-all-start) | async-done | bytes 65568 | tf_op jit(solution)/shard_map/all_to_all | solution.py:285
  97.3 15.7 %all-to-all-start.1 = ((f32[16,1,1024]{2,1,0:T(1,128)}), f32[16,1,1024]{2,1,0:T(1,128)S(1)}, u32[]{:S(2)}, u32[]{:S(2)}) async-start(f32[16,1,1024]{2,1,0:T(1,128)} %reshape.3406), calls=%async_computation.1 | async-start | bytes 131072 | tf_op jit(solution)/shard_map/all_to_all | solution.py:292
  113.2 9.9 %all-to-all-done.1 = f32[16,1,1024]{2,1,0:T(1,128)S(1)} async-done(((f32[16,1,1024]{2,1,0:T(1,128)}), f32[16,1,1024]{2,1,0:T(1,128)S(1)}, u32[]{:S(2)}, u32[]{:S(2)}) %all-to-all-start.1) | async-done | bytes 65568 | tf_op jit(solution)/shard_map/all_to_all | solution.py:292
  150.9 16.2 %collective-permute-start.3 = (f32[3,1,4,512]{3,2,1,0:T(4,128)S(1)}, f32[3,1,4,512]{3,2,1,0:T(4,128)S(1)}, u32[]{:S(2)}, u32[]{:S(2)}) collective-permute-start(f32[3,1,4,512]{3,2,1,0:T(4,128)S(1)} %pad_maximum_fusion.19), channel_id=1, source_target_pairs={{1,0},{2,1},{3,2},{4,3},{5,4},{6,5},{7,6},{8,7},{9,8},{10,9},{11,1... | collective-permute-start | bytes 73736 | tf_op jit(solution)/shard_map/ppermute | solution.py:31
  169.1 16.3 %collective-permute-start.7 = (f32[3,1,2,3,512]{4,2,3,1,0:T(2,128)S(1)}, f32[3,1,2,3,512]{4,2,3,1,0:T(2,128)S(1)}, u32[]{:S(2)}, u32[]{:S(2)}) collective-permute-start(f32[3,1,2,3,512]{4,2,3,1,0:T(2,128)S(1)} %pad_maximum_fusion.17), channel_id=1, source_target_pairs={{1,0},{2,1},{3,2},{4,3},{5,4},{6,5},{7,6},{8,7},{9,8},{10,9},{11,1... | collective-permute-start | bytes 110600 | tf_op jit(solution)/shard_map/ppermute | solution.py:31
  208.2 16.3 %collective-permute-start.15 = (f32[2,12,2,256]{3,1,2,0:T(8,128)}, f32[2,12,2,256]{3,1,2,0:T(8,128)}, u32[]{:S(2)}, u32[]{:S(2)}) collective-permute-start(f32[2,12,2,256]{3,1,2,0:T(8,128)} %get-tuple-element.277), channel_id=1, source_target_pairs={{1,0},{2,1},{3,2},{4,3},{5,4},{6,5},{7,6},{8,7},{9,8},{10,9},{11,1... | collective-permute-start | bytes 147464 | tf_op jit(solution)/shard_map/ppermute | solution.py:31
  228.0 64.6 %while.22 = (s32[]{:T(128)}, f32[4,2,3,128]{3,2,1,0:T(4,128)}, s32[4]{0:T(128)}, s32[4,12]{1,0:T(4,128)}, f32[36,4,128]{2,1,0:T(4,128)}, /*index=5*/f32[4,4,128]...) while((s32[]{:T(128)}, f32[4,2,3,128]{3,2,1,0:T(4,128)}, ...), condition=%wide.region_7.8_spmd.clone, body=%wide.region_2.7_spmd.sunk.clone.sunk | while | flops 31867188 | bytes 20759720 | solution.py:245
  296.8 111.2 %all-reduce.14 = (f32[2]{0:T(128)S(1)}, f32[2]{0:T(128)S(1)}) all-reduce(f32[2]{0:T(128)S(1)} %get-tuple-element.189, f32[2]{0:T(128)S(1)} %get-tuple-element.188), channel_id=1, replica_groups=mesh['row'=16,'col'=32] {'row','col'}, use_global_device_ids=true, to_apply=%region_1.2 | all-reduce | flops 4 | bytes 32 | tf_op jit(solution)/shard_map/psum | solution.py:174
  408.2 102.5 %psum.30 = f32[2]{0:T(128)S(1)} all-reduce(f32[2]{0:T(128)S(1)} %get-tuple-element.226), channel_id=1, replica_groups=mesh['row'=16,'col'=32] {'row','col'}, use_global_device_ids=true, to_apply=%region_14.15 | all-reduce | flops 2 | bytes 16 | tf_op jit(solution)/shard_map/psum | solution.py:174
  522.4 6.6 collective-permute-start.23
  531.2 17.4 %collective-permute-done.22 = f32[2,16,2,256]{3,2,1,0:T(2,128)S(1)} collective-permute-done((f32[2,16,2,256]{3,2,1,0:T(2,128)S(1)}, f32[2,16,2,256]{3,2,1,0:T(2,128)S(1)}, u32[]{:S(2)}, u32[]{:S(2)}) %collective-permute-start.22) | collective-permute-done | bytes 65568 | tf_op jit(solution)/shard_map/ppermute | solution.py:29
  551.9 21.8 %all_to_all.144 = f32[32,1,512]{2,1,0:T(1,128)S(1)} all-to-all(f32[32,1,512]{2,1,0:T(1,128)S(1)} %reshape.3412), channel_id=1, replica_groups=mesh['row'=16,'col'=32] {'col'}, dimensions={0} | all-to-all | bytes 131072 | tf_op jit(solution)/shard_map/all_to_all | solution.py:285
  579.1 24.4 %all_to_all.145 = f32[16,1,1024]{2,1,0:T(1,128)S(1)} all-to-all(f32[16,1,1024]{2,1,0:T(1,128)S(1)} %reshape.3414), channel_id=1, replica_groups=mesh['row'=16,'col'=32] {'row'}, dimensions={0} | all-to-all | bytes 131072 | tf_op jit(solution)/shard_map/all_to_all | solution.py:292
  613.1 10.0 %all-to-all-done.6 = f32[16,1,1024]{2,1,0:T(1,128)S(1)} async-done(((f32[16,1,1024]{2,1,0:T(1,128)}), f32[16,1,1024]{2,1,0:T(1,128)S(1)}, u32[]{:S(2)}, u32[]{:S(2)}) %all-to-all-start.6) | async-done | bytes 65568 | tf_op jit(solution)/shard_map/all_to_all | solution.py:299
  639.1 16.2 %collective-permute-start.19 = (f32[3,1,2,3,512]{4,2,3,1,0:T(2,128)S(1)}, f32[3,1,2,3,512]{4,2,3,1,0:T(2,128)S(1)}, u32[]{:S(2)}, u32[]{:S(2)}) collective-permute-start(f32[3,1,2,3,512]{4,2,3,1,0:T(2,128)S(1)} %pad_maximum_fusion.18), channel_id=1, source_target_pairs={{1,0},{2,1},{3,2},{4,3},{5,4},{6,5},{7,6},{8,7},{9,8},{10,9},{11,1... | collective-permute-start | bytes 110600 | tf_op jit(solution)/shard_map/ppermute | solution.py:31
  661.0 11.2 %collective-permute-start.25 = (f32[2,2,4,256]{3,1,2,0:T(2,128)S(1)}, f32[2,2,4,256]{3,1,2,0:T(2,128)S(1)}, u32[]{:S(2)}, u32[]{:S(2)}) collective-permute-start(f32[2,2,4,256]{3,1,2,0:T(2,128)S(1)} %get-tuple-element.279), channel_id=1, source_target_pairs={{32,0},{64,32},{96,64},{128,96},{160,128},{192,160},{224,192},{256... | collective-permute-start | bytes 49160 | tf_op jit(solution)/shard_map/ppermute | solution.py:31
  676.0 16.6 %collective-permute-start.27 = (f32[2,12,2,256]{3,1,2,0:T(8,128)}, f32[2,12,2,256]{3,1,2,0:T(8,128)}, u32[]{:S(2)}, u32[]{:S(2)}) collective-permute-start(f32[2,12,2,256]{3,1,2,0:T(8,128)} %get-tuple-element.275), channel_id=1, source_target_pairs={{1,0},{2,1},{3,2},{4,3},{5,4},{6,5},{7,6},{8,7},{9,8},{10,9},{11,1... | collective-permute-start | bytes 147464 | tf_op jit(solution)/shard_map/ppermute | solution.py:31
  695.9 67.4 %while.23 = (s32[]{:T(128)}, f32[4,2,3,128]{3,2,1,0:T(4,128)}, s32[4]{0:T(128)}, s32[4,12]{1,0:T(4,128)}, f32[36,4,128]{2,1,0:T(4,128)}, /*index=5*/f32[4,4,128]...) while((s32[]{:T(128)}, f32[4,2,3,128]{3,2,1,0:T(4,128)}, ...), condition=%wide.region_20.21_spmd.clone, body=%wide.region_15.20_spmd.sunk.clone.sunk | while | flops 31867188 | bytes 20759552 | solution.py:245
  767.6 110.7 %psum.31 = f32[2]{0:T(128)S(1)} all-reduce(f32[2]{0:T(128)S(1)} %multiply_reduce_fusion.12), channel_id=1, replica_groups=mesh['row'=16,'col'=32] {'row','col'}, use_global_device_ids=true, to_apply=%region_25.26 | all-reduce | flops 2 | bytes 16 | tf_op jit(solution)/shard_map/psum | solution.py:174
  (509 shorter events, 268.6 us)
Async XLA Ops:
  2.0 148.9 %collective-permute-start.1 = (f32[1,1,4,512]{3,2,1,0:T(4,128)S(1)}, f32[1,1,4,512]{3,2,1,0:T(4,128)S(1)}, u32[]{:S(2)}, u32[]{:S(2)}) collective-permute-start(f32[1,1,4,512]{3,2,1,0:T(4,128)S(1)} %maximum_bitcast_fusion.5), channel_id=1, source_target_pairs={{32,0},{64,32},{96,64},{128,96},{160,128},{192,160},{224,192},{256... | collective-permute-start | bytes 24584 | tf_op jit(solution)/shard_map/ppermute | solution.py:31
  10.8 140.1 %collective-permute-start = (f32[1,1,4,512]{3,2,1,0:T(4,128)S(1)}, f32[1,1,4,512]{3,2,1,0:T(4,128)S(1)}, u32[]{:S(2)}, u32[]{:S(2)}) collective-permute-start(f32[1,1,4,512]{3,2,1,0:T(4,128)S(1)} %maximum_bitcast_fusion.5), channel_id=1, source_target_pairs={{0,32},{32,64},{64,96},{96,128},{128,160},{160,192},{192,224},{224... | collective-permute-start | bytes 24584 | tf_op jit(solution)/shard_map/ppermute | solution.py:29
  36.3 14.5 %collective-permute-start.11 = (f32[2,16,2,256]{3,2,1,0:T(2,128)S(1)}, f32[2,16,2,256]{3,2,1,0:T(2,128)S(1)}, u32[]{:S(2)}, u32[]{:S(2)}) collective-permute-start(f32[2,16,2,256]{3,2,1,0:T(2,128)S(1)} %get-tuple-element.269), channel_id=1, source_target_pairs={{1,0},{2,1},{3,2},{4,3},{5,4},{6,5},{7,6},{8,7},{9,8},{10,9},{11,1... | collective-permute-start | bytes 196616 | tf_op jit(solution)/shard_map/ppermute | solution.py:31
  48.9 17.9 %collective-permute-start.10 = (f32[2,16,2,256]{3,2,1,0:T(2,128)S(1)}, f32[2,16,2,256]{3,2,1,0:T(2,128)S(1)}, u32[]{:S(2)}, u32[]{:S(2)}) collective-permute-start(f32[2,16,2,256]{3,2,1,0:T(2,128)S(1)} %get-tuple-element.268), channel_id=1, source_target_pairs={{0,1},{1,2},{2,3},{3,4},{4,5},{5,6},{6,7},{7,8},{8,9},{9,10},{10,1... | collective-permute-start | bytes 196616 | tf_op jit(solution)/shard_map/ppermute | solution.py:29
  70.8 20.0 %all-to-all-start = ((f32[32,1,512]{2,1,0:T(1,128)}), f32[32,1,512]{2,1,0:T(1,128)S(1)}, u32[]{:S(2)}, u32[]{:S(2)}) async-start(f32[32,1,512]{2,1,0:T(1,128)} %reshape.3404), calls=%async_computation | async-start | bytes 131072 | tf_op jit(solution)/shard_map/all_to_all | solution.py:285
  97.3 25.8 %all-to-all-start.1 = ((f32[16,1,1024]{2,1,0:T(1,128)}), f32[16,1,1024]{2,1,0:T(1,128)S(1)}, u32[]{:S(2)}, u32[]{:S(2)}) async-start(f32[16,1,1024]{2,1,0:T(1,128)} %reshape.3406), calls=%async_computation.1 | async-start | bytes 131072 | tf_op jit(solution)/shard_map/all_to_all | solution.py:292
  128.1 14.4 %all-to-all-start.2 = ((f32[16,1,1024]{2,1,0:T(1,128)}), f32[16,1,1024]{2,1,0:T(1,128)S(1)}, u32[]{:S(2)}, u32[]{:S(2)}) async-start(f32[16,1,1024]{2,1,0:T(1,128)} %reshape.3408), calls=%async_computation.2 | async-start | bytes 131072 | tf_op jit(solution)/shard_map/all_to_all | solution.py:299
  132.4 36.6 %collective-permute-start.5 = (f32[1,1,2,3,512]{4,2,3,1,0:T(2,128)S(1)}, f32[1,1,2,3,512]{4,2,3,1,0:T(2,128)S(1)}, u32[]{:S(2)}, u32[]{:S(2)}) collective-permute-start(f32[1,1,2,3,512]{4,2,3,1,0:T(2,128)S(1)} %broadcast_multiply_fusion.9), channel_id=1, source_target_pairs={{32,0},{64,32},{96,64},{128,96},{160,128},{192,160},{224,192},{256... | collective-permute-start | bytes 36872 | tf_op jit(solution)/shard_map/ppermute | solution.py:31
  134.6 34.5 %collective-permute-start.4 = (f32[1,1,2,3,512]{4,2,3,1,0:T(2,128)S(1)}, f32[1,1,2,3,512]{4,2,3,1,0:T(2,128)S(1)}, u32[]{:S(2)}, u32[]{:S(2)}) collective-permute-start(f32[1,1,2,3,512]{4,2,3,1,0:T(2,128)S(1)} %broadcast_multiply_fusion.9), channel_id=1, source_target_pairs={{0,32},{32,64},{64,96},{96,128},{128,160},{160,192},{192,224},{224... | collective-permute-start | bytes 36872 | tf_op jit(solution)/shard_map/ppermute | solution.py:29
  147.0 41.0 %all-to-all-start.3 = ((f32[32,1,512]{2,1,0:T(1,128)}), f32[32,1,512]{2,1,0:T(1,128)S(1)}, u32[]{:S(2)}, u32[]{:S(2)}) async-start(f32[32,1,512]{2,1,0:T(1,128)} %reshape.3410), calls=%async_computation.3 | async-start | bytes 131072 | tf_op jit(solution)/shard_map/all_to_all | solution.py:301
  150.9 36.4 %collective-permute-start.3 = (f32[3,1,4,512]{3,2,1,0:T(4,128)S(1)}, f32[3,1,4,512]{3,2,1,0:T(4,128)S(1)}, u32[]{:S(2)}, u32[]{:S(2)}) collective-permute-start(f32[3,1,4,512]{3,2,1,0:T(4,128)S(1)} %pad_maximum_fusion.19), channel_id=1, source_target_pairs={{1,0},{2,1},{3,2},{4,3},{5,4},{6,5},{7,6},{8,7},{9,8},{10,9},{11,1... | collective-permute-start | bytes 73736 | tf_op jit(solution)/shard_map/ppermute | solution.py:31
  167.1 20.2 %collective-permute-start.2 = (f32[3,1,4,512]{3,2,1,0:T(4,128)S(1)}, f32[3,1,4,512]{3,2,1,0:T(4,128)S(1)}, u32[]{:S(2)}, u32[]{:S(2)}) collective-permute-start(f32[3,1,4,512]{3,2,1,0:T(4,128)S(1)} %pad_maximum_fusion.19), channel_id=1, source_target_pairs={{0,1},{1,2},{2,3},{3,4},{4,5},{5,6},{6,7},{7,8},{8,9},{9,10},{10,1... | collective-permute-start | bytes 73736 | tf_op jit(solution)/shard_map/ppermute | solution.py:29
  169.1 30.6 %collective-permute-start.7 = (f32[3,1,2,3,512]{4,2,3,1,0:T(2,128)S(1)}, f32[3,1,2,3,512]{4,2,3,1,0:T(2,128)S(1)}, u32[]{:S(2)}, u32[]{:S(2)}) collective-permute-start(f32[3,1,2,3,512]{4,2,3,1,0:T(2,128)S(1)} %pad_maximum_fusion.17), channel_id=1, source_target_pairs={{1,0},{2,1},{3,2},{4,3},{5,4},{6,5},{7,6},{8,7},{9,8},{10,9},{11,1... | collective-permute-start | bytes 110600 | tf_op jit(solution)/shard_map/ppermute | solution.py:31
  185.4 17.7 %collective-permute-start.6 = (f32[3,1,2,3,512]{4,2,3,1,0:T(2,128)S(1)}, f32[3,1,2,3,512]{4,2,3,1,0:T(2,128)S(1)}, u32[]{:S(2)}, u32[]{:S(2)}) collective-permute-start(f32[3,1,2,3,512]{4,2,3,1,0:T(2,128)S(1)} %pad_maximum_fusion.17), channel_id=1, source_target_pairs={{0,1},{1,2},{2,3},{3,4},{4,5},{5,6},{6,7},{7,8},{8,9},{9,10},{10,1... | collective-permute-start | bytes 110600 | tf_op jit(solution)/shard_map/ppermute | solution.py:29
  208.2 85.1 %collective-permute-start.15 = (f32[2,12,2,256]{3,1,2,0:T(8,128)}, f32[2,12,2,256]{3,1,2,0:T(8,128)}, u32[]{:S(2)}, u32[]{:S(2)}) collective-permute-start(f32[2,12,2,256]{3,1,2,0:T(8,128)} %get-tuple-element.277), channel_id=1, source_target_pairs={{1,0},{2,1},{3,2},{4,3},{5,4},{6,5},{7,6},{8,7},{9,8},{10,9},{11,1... | collective-permute-start | bytes 147464 | tf_op jit(solution)/shard_map/ppermute | solution.py:31
  224.5 68.9 %collective-permute-start.14 = (f32[2,12,2,256]{3,1,2,0:T(8,128)}, f32[2,12,2,256]{3,1,2,0:T(8,128)}, u32[]{:S(2)}, u32[]{:S(2)}) collective-permute-start(f32[2,12,2,256]{3,1,2,0:T(8,128)} %get-tuple-element.276), channel_id=1, source_target_pairs={{0,1},{1,2},{2,3},{3,4},{4,5},{5,6},{6,7},{7,8},{8,9},{9,10},{10,1... | collective-permute-start | bytes 147464 | tf_op jit(solution)/shard_map/ppermute | solution.py:29
  529.1 19.5 %collective-permute-start.22 = (f32[2,16,2,256]{3,2,1,0:T(2,128)S(1)}, f32[2,16,2,256]{3,2,1,0:T(2,128)S(1)}, u32[]{:S(2)}, u32[]{:S(2)}) collective-permute-start(f32[2,16,2,256]{3,2,1,0:T(2,128)S(1)} %get-tuple-element.260), channel_id=1, source_target_pairs={{0,1},{1,2},{2,3},{3,4},{4,5},{5,6},{6,7},{7,8},{8,9},{9,10},{10,1... | collective-permute-start | bytes 196616 | tf_op jit(solution)/shard_map/ppermute | solution.py:29
  608.5 14.6 %all-to-all-start.6 = ((f32[16,1,1024]{2,1,0:T(1,128)}), f32[16,1,1024]{2,1,0:T(1,128)S(1)}, u32[]{:S(2)}, u32[]{:S(2)}) async-start(f32[16,1,1024]{2,1,0:T(1,128)} %reshape.3416), calls=%async_computation.6 | async-start | bytes 131072 | tf_op jit(solution)/shard_map/all_to_all | solution.py:299
  627.6 29.6 %all-to-all-start.7 = ((f32[32,1,512]{2,1,0:T(1,128)}), f32[32,1,512]{2,1,0:T(1,128)S(1)}, u32[]{:S(2)}, u32[]{:S(2)}) async-start(f32[32,1,512]{2,1,0:T(1,128)} %reshape.3418), calls=%async_computation.7 | async-start | bytes 131072 | tf_op jit(solution)/shard_map/all_to_all | solution.py:301
  639.1 35.1 %collective-permute-start.19 = (f32[3,1,2,3,512]{4,2,3,1,0:T(2,128)S(1)}, f32[3,1,2,3,512]{4,2,3,1,0:T(2,128)S(1)}, u32[]{:S(2)}, u32[]{:S(2)}) collective-permute-start(f32[3,1,2,3,512]{4,2,3,1,0:T(2,128)S(1)} %pad_maximum_fusion.18), channel_id=1, source_target_pairs={{1,0},{2,1},{3,2},{4,3},{5,4},{6,5},{7,6},{8,7},{9,8},{10,9},{11,1... | collective-permute-start | bytes 110600 | tf_op jit(solution)/shard_map/ppermute | solution.py:31
  655.2 19.0 %collective-permute-start.18 = (f32[3,1,2,3,512]{4,2,3,1,0:T(2,128)S(1)}, f32[3,1,2,3,512]{4,2,3,1,0:T(2,128)S(1)}, u32[]{:S(2)}, u32[]{:S(2)}) collective-permute-start(f32[3,1,2,3,512]{4,2,3,1,0:T(2,128)S(1)} %pad_maximum_fusion.18), channel_id=1, source_target_pairs={{0,1},{1,2},{2,3},{3,4},{4,5},{5,6},{6,7},{7,8},{8,9},{9,10},{10,1... | collective-permute-start | bytes 110600 | tf_op jit(solution)/shard_map/ppermute | solution.py:29
  661.0 14.1 %collective-permute-start.25 = (f32[2,2,4,256]{3,1,2,0:T(2,128)S(1)}, f32[2,2,4,256]{3,1,2,0:T(2,128)S(1)}, u32[]{:S(2)}, u32[]{:S(2)}) collective-permute-start(f32[2,2,4,256]{3,1,2,0:T(2,128)S(1)} %get-tuple-element.279), channel_id=1, source_target_pairs={{32,0},{64,32},{96,64},{128,96},{160,128},{192,160},{224,192},{256... | collective-permute-start | bytes 49160 | tf_op jit(solution)/shard_map/ppermute | solution.py:31
  676.0 88.1 %collective-permute-start.27 = (f32[2,12,2,256]{3,1,2,0:T(8,128)}, f32[2,12,2,256]{3,1,2,0:T(8,128)}, u32[]{:S(2)}, u32[]{:S(2)}) collective-permute-start(f32[2,12,2,256]{3,1,2,0:T(8,128)} %get-tuple-element.275), channel_id=1, source_target_pairs={{1,0},{2,1},{3,2},{4,3},{5,4},{6,5},{7,6},{8,7},{9,8},{10,9},{11,1... | collective-permute-start | bytes 147464 | tf_op jit(solution)/shard_map/ppermute | solution.py:31
  692.6 71.6 %collective-permute-start.26 = (f32[2,12,2,256]{3,1,2,0:T(8,128)}, f32[2,12,2,256]{3,1,2,0:T(8,128)}, u32[]{:S(2)}, u32[]{:S(2)}) collective-permute-start(f32[2,12,2,256]{3,1,2,0:T(8,128)} %get-tuple-element.274), channel_id=1, source_target_pairs={{0,1},{1,2},{2,3},{3,4},{4,5},{5,6},{6,7},{7,8},{8,9},{9,10},{10,1... | collective-permute-start | bytes 147464 | tf_op jit(solution)/shard_map/ppermute | solution.py:29
  (64 other events, 1641.3 us)
where the time goes:
time: 891 us; the launch traced here: 879 us
  blocking collectives  371 us (42%)
  starting transfers between devices  209 us (23%)
  waiting for transfers between devices  94.4 us (11%)
  other arithmetic  92.1 us (10%)
  local copies, waits for them, and re-layouts  77.2 us (9%)
  matrix products  17.6 us (2%)
  loops' own time  15.9 us (2%)
    psum x3, blocking collectives, inner_sum(): return lax.psum(jnp.sum(left_arr * right_arr, axis=(1, 2)), ('row', 'col'))  324 us
    ppermute x14, starting transfers between devices, with_halo(): lax.ppermute(head, axis, [((i + 1) % count, i) for i in range(count)])  141 us
    ppermute x14, waiting for transfers between devices, with_halo(): lax.ppermute(tail, axis, [(i, (i + 1) % count) for i in range(count)])  54.6 us
    ppermute x14, starting transfers between devices, with_halo(): lax.ppermute(tail, axis, [(i, (i + 1) % count) for i in range(count)])  31 us
    all_to_all x1, blocking collectives, local(): lax.all_to_all(along_y, 'row', split_axis=2, concat_axis=1, tiled=True)  24.4 us
    all_to_all x1, blocking collectives, local(): lax.all_to_all(spectrum, 'col', split_axis=3, concat_axis=2, tiled=True)  21.8 us
    select_n x8, other arithmetic, tile_field(): second = jnp.where(itself, 0.0, second)  20.7 us
  transfers between devices with their start and end apart: 34, of which 12 were waited for; matrix products, arithmetic and copies ran while one was open for 18% of the time, Pallas kernels for 0%

commit v1 on v0

v1 whole, which is shorter than its diff:
```python
import functools
import math

import jax
import jax.numpy as jnp
import numpy as np
from jax import lax
from jax.experimental import pallas as pl
from jax.experimental.pallas import tpu as pltpu
from jax.sharding import PartitionSpec as P

MESH = pl.DeviceIdType.MESH
CX = 8
CY = 4
KZ = 256
TILE = 128
TILES = 4
NBR = 12
ATOMS = TILE * TILES
ROWS = 16
COLS = 32
GX = CX * ROWS
GY = CY * COLS
LANES = 128

BETA = 0.4
THOLE = 0.39
SELF = 4.0 * BETA**3 / (3.0 * math.sqrt(math.pi))
ERFCX = (
    0.22567586600780487,
    0.2256697714328766,
    0.20783858001232147,
    0.16857817769050598,
    0.14127734303474426,
    -0.005255409982055426,
    0.16864386200904846,
    -0.18261533975601196,
    0.05018728971481323,
)

NEIGHBOURS = [(dr, dc) for dr in (-1, 0, 1) for dc in (-1, 0, 1) if (dr, dc) != (0, 0)]
ROW_STEP = {-1: ROWS - 1, 0: 0, 1: 1}
COL_STEP = {-1: COLS - 1, 0: 0, 1: 1}


def region_rows():
    rows = [(x, y, s) for y in range(CY) for s in range(2) for x in range(CX)]
    cuts = {}
    for dr, dc in NEIGHBOURS:
        first = len(rows)
        xs = {-1: [-2, -1], 0: list(range(CX)), 1: [CX, CX + 1]}[dr]
        ys = {-1: [-2, -1], 0: list(range(CY)), 1: [CY, CY + 1]}[dc]
        rows += [(x, y, s) for s in range(2) for y in ys for x in xs]
        cuts[dr, dc] = (first, len(rows) - first)
    return rows, cuts


REGION, CUTS = region_rows()
CENTRE = 2 * CX * CY
ALL = len(REGION)
OUTER = ALL - CENTRE
GROUP_S = []
for _g in range(ALL // 8):
    _s = [REGION[8 * _g + _k][2] for _k in range(8)]
    GROUP_S.append(_s[0] if _s[0] == _s[7] else 2)


def cas(rows, cols, length):
    angle = 2.0 * np.pi / length * ((rows[:, None] * cols[None, :]) % length)
    return (np.cos(angle) + np.sin(angle)).astype(np.float32)


def wave_tables(length):
    k = np.arange(length)
    f = np.minimum(k, length - k) / length
    c = np.array([1.0, 11.0, 11.0, 1.0]) / 24.0
    angle = 2.0 * np.pi / length * ((k[:, None] * np.arange(4)[None, :]) % length)
    b = (np.cos(angle) @ c) ** 2 + (np.sin(angle) @ c) ** 2
    inverse = np.where(2 * k == length, 0.0, 1.0 / np.where(2 * k == length, 1.0, b))
    return (f * f), inverse


def constants():
    q = np.arange(KZ)
    h, cp, i = q // 128, q % 128 // 8, q % 8
    wave_z = 16 * cp + 8 * h + i
    hz = cas(wave_z, np.arange(KZ), KZ)
    hy = cas(np.arange(GY), np.arange(GY), GY)
    hx = cas(np.arange(GX), np.arange(GX), GX)
    lane = {(hh, y, s, x): ((hh * CY + y) * 2 + s) * CX + x for hh in range(2) for y in range(CY) for s in range(2) for x in range(CX)}
    place = np.zeros((2, ALL, LANES), np.float32)
    for row, (x, y, s) in enumerate(REGION):
        for hh in range(2):
            place[hh, row, lane[hh, y % CY, s, x % CX]] = 1.0
    cells = np.zeros((2, ALL, LANES), np.int32)
    for row, (x, y, s) in enumerate(REGION):
        cells[0, row] = x
        cells[1, row] = y
    fx, bx = wave_tables(GX)
    fy, by = wave_tables(GY)
    fz, bz = wave_tables(KZ)
    scale = 1.0 / (GX * GY * KZ * math.pi)
    lanes = np.arange(LANES)
    lane_i, lane_ky = lanes // 16, lanes % 8
    fx_rows = np.broadcast_to(np.stack([fx, bx * scale])[:, :, None], (2, GX, LANES)).astype(np.float32)
    wave_y = 8 * np.arange(ROWS)[:, None] + lane_ky[None, :]
    fy_rows = np.stack([fy[wave_y], by[wave_y]]).astype(np.float32)
    wave = 8 * np.arange(COLS)[:, None] + lane_i[None, :]
    fz_rows = np.stack([fz[wave], bz[wave]]).astype(np.float32)
    return hz, hy, hx, place, cells, fx_rows, fy_rows, fz_rows


def mm(a, b, dims=((1,), (0,))):
    return lax.dot_general(
        a, b, (dims, ((), ())), precision=lax.Precision.HIGHEST, preferred_element_type=jnp.float32
    )


def swap_bits(v, unit):
    sub = lax.broadcasted_iota(jnp.int32, v.shape, 1)
    lane = lax.broadcasted_iota(jnp.int32, v.shape, 2) // unit
    for k in (1, 2, 4):
        if k == 4:
            moved = pltpu.roll(v, 4, 1)
        else:
            moved = jnp.where(sub & k == 0, pltpu.roll(v, 8 - k, 1), pltpu.roll(v, k, 1))
        if k * unit * 2 == LANES:
            moved = pltpu.roll(moved, k * unit, 2)
        else:
            moved = jnp.where(
                lane & k == 0, pltpu.roll(moved, LANES - k * unit, 2), pltpu.roll(moved, k * unit, 2)
            )
        v = jnp.where(sub & k == lane & k, v, moved)
    return v


def spline(fraction):
    previous = {0: jnp.ones_like(fraction)}
    fourth = previous
    for degree in range(2, 6):
        current = {}
        for offset in range(degree):
            abscissa = fraction + float(offset)
            summed = (float(degree) - abscissa) * previous[offset - 1] if offset else None
            if offset in previous:
                term = abscissa * previous[offset]
                summed = term if summed is None else term + summed
            current[offset] = summed * (1.0 / (degree - 1))
        if degree == 4:
            fourth = current
        previous = current
    values = [previous[4 - j] for j in range(5)]
    slopes = []
    for j in range(5):
        low = fourth.get(4 - j)
        high = fourth.get(3 - j)
        slopes.append(-high if low is None else low if high is None else low - high)
    return values, slopes


def kernel(
    field, place, polar, base, lists, hz, hy, hx, mt, cells, fx, fy, fz,
    out_x, out_r,
    pdx, pdy, pdf, zhat, zhat_t, infl, own, coef, acc, direct, vec, rowbuf,
    dsend0, dsend1, near0, near1, hsend, hrecv, csend, crecv, rsend, rrecv, ssend, srecv, tsend, trecv,
    gsend, grecv, psend, pcol, psend2, prow,
    send_sem, recv_sem,
):
    me_r = lax.axis_index("row")
    me_c = lax.axis_index("col")

    def to(dr, dc):
        return (lax.rem(me_r + ROW_STEP[dr], ROWS), lax.rem(me_c + COL_STEP[dc], COLS))

    barrier = pltpu.get_barrier_semaphore()

    @pl.loop(1, COLS)
    def _(k):
        pl.semaphore_signal(barrier, 1, device_id=(me_r, lax.rem(me_c + k, COLS)), device_id_type=MESH)

    @pl.loop(1, ROWS)
    def _(k):
        pl.semaphore_signal(barrier, 1, device_id=(lax.rem(me_r + k, ROWS), me_c), device_id_type=MESH)

    for dr, dc in NEIGHBOURS:
        if dr and dc:
            pl.semaphore_signal(barrier, 1, device_id=to(dr, dc), device_id_type=MESH)

    def remote(src, dst, phase, device):
        pltpu.make_async_remote_copy(
            src_ref=src, dst_ref=dst, send_sem=send_sem.at[phase], recv_sem=recv_sem.at[phase],
            device_id=device, device_id_type=MESH,
        ).start()

    def keep(src, dst, phase):
        pltpu.make_async_copy(src, dst, recv_sem.at[phase]).start()

    def arrived(ref, phase):
        pltpu.make_async_copy(ref, ref, recv_sem.at[phase]).wait()

    def left(ref, phase):
        pltpu.make_async_copy(ref, ref, send_sem.at[phase]).wait()

    def rows6(ref):
        vec[...] = jnp.zeros((8, ATOMS), jnp.float32)
        vec[0:3, :] = ref[0, 0, 0]
        vec[3:6, :] = ref[0, 0, 1]
        return vec[...]

    row_id = lax.broadcasted_iota(jnp.int32, (8, ATOMS), 0)
    first_half = row_id < 4
    alpha = polar[0, 0:1, 0, :]
    r0 = rows6(field)
    d1 = alpha * r0

    iroot = jnp.exp(jnp.log(alpha) * (-1.0 / 6.0))
    vec[0:3, :] = place[0, 0]
    vec[3:4, :] = iroot
    vec[4:8, :] = jnp.zeros((4, ATOMS), jnp.float32)
    for t in range(TILES):
        cut = slice(t * TILE, (t + 1) * TILE)
        dsend0[t, 0:8, :] = vec[:, cut]
        dsend0[t, 8:16, :] = d1[:, cut]
    pl.semaphore_wait(barrier, COLS - 1 + ROWS - 1 + 4)

    def send_near(src, dst, phase):
        for dr, dc in NEIGHBOURS:
            slot = (1 - dr) * 3 + (1 - dc)
            remote(src, dst.at[pl.ds(slot * TILES, TILES)], phase, to(dr, dc))
        keep(src, dst.at[pl.ds(4 * TILES, TILES)], phase)

    send_near(dsend0, near0, 0)

    vec[0:3, :] = place[0, 0]
    vec[3:8, :] = jnp.zeros((5, ATOMS), jnp.float32)
    cell = base[0, 0] + 2
    axis_row = lax.broadcasted_iota(jnp.int32, (3, ATOMS), 0)
    cell = cell & jnp.where(axis_row == 2, KZ - 1, GX - 1)
    fraction = place[0, 0] - cell.astype(jnp.float32)
    values, slopes = spline(fraction)
    base_all = base[0, 0]
    rel_x = ((base_all[0:1] - me_r * CX + 2) & (GX - 1)) - 2
    rel_y = ((base_all[1:2] - me_c * CY + 2) & (GY - 1)) - 2
    rel_z = base_all[2:3]

    def placed(step, row):
        value = jnp.zeros(step.shape, jnp.float32)
        slope = jnp.zeros(step.shape, jnp.float32)
        for j in range(5):
            here = step == j
            value = jnp.where(here, values[j][row : row + 1], value)
            slope = jnp.where(here, slopes[j][row : row + 1], slope)
        return value, slope

    for g in range(ALL // 32):
        cut = slice(32 * g, 32 * g + 32)
        cell_x = jnp.concatenate([cells[0, cut, :]] * TILES, axis=1)
        cell_y = jnp.concatenate([cells[1, cut, :]] * TILES, axis=1)
        tx, sx = placed(cell_x - rel_x, 0)
        ty, sy = placed(cell_y - rel_y, 1)
        pdx[cut, :] = sx * ty
        pdy[cut, :] = tx * sy
        pdf[cut, :] = tx * ty
    step_z = (lax.broadcasted_iota(jnp.int32, (KZ, ATOMS), 0) - rel_z) & (KZ - 1)
    tz, sz = placed(step_z, 2)
    zhat[:, 0:ATOMS] = mm(hz[...], tz)
    zhat[:, ATOMS:] = mm(hz[...], sz)
    zhat_t[...] = zhat[...].T

    row_y = fy[:, pl.ds(me_r, 1), :]
    row_z = fz[:, pl.ds(me_c, 1), :]
    m2 = fx[0] + (row_y[0] + row_z[0])
    zero = m2 == 0.0
    safe = jnp.where(zero, 1.0, m2)
    shape = jnp.exp(-(math.pi**2 / BETA**2) * safe) / safe * (fx[1] * (row_y[1] * row_z[1]))
    infl[...] = jnp.where(zero, 0.0, shape)

    for t in range(TILES):
        cut = slice(t * TILE, (t + 1) * TILE)
        for c in range(4):
            source = iroot[:, cut] if c == 3 else place[0, 0, c : c + 1, cut]
            own[t, c] = jnp.broadcast_to(source, (TILE, TILE)).T

    block = 16
    blocks = TILE // block

    def pair_unit(op, unit):
        t = unit // blocks
        first = pl.multiple_of((unit - t * blocks) * block, block)
        cut = pl.ds(first, block)
        lane = lax.broadcasted_iota(jnp.int32, (block, TILE), 1)
        line = lax.broadcasted_iota(jnp.int32, (block, TILE), 0) + first

        def body(k, sums):
            entry = lists[0, 0, t, k]
            at = t * NBR + k
            if op == 0:
                near = near0[entry]
                dip = near[8:16]
                delta = []
                for c, span in ((0, GX), (1, GY), (2, KZ)):
                    d = near[c : c + 1] - own[t, c, cut, :]
                    delta.append(d - float(span) * jnp.floor(d * (1.0 / span) + 0.5))
                dx, dy, dz = delta
                sq = dx * dx + dy * dy + dz * dz
                itself = line + k * TILE == lane
                sq = jnp.where(itself, 1.0, sq)
                inv = lax.rsqrt(sq)
                rho = sq * inv
                scaled = rho * (own[t, 3, cut, :] * near[3:4])
                u3 = THOLE * (scaled * scaled * scaled)
                damp = jnp.exp(-u3)
                gauss = jnp.exp(-(BETA * BETA) * sq)
                t_ = 1.0 / (1.0 + (0.4 * BETA) * rho)
                poly = jnp.full_like(t_, ERFCX[-1])
                for c in ERFCX[-2::-1]:
                    poly = poly * t_ + c
                screen = gauss * (t_ * poly)
                g = (2.0 * BETA / math.sqrt(math.pi)) * gauss
                i2 = inv * inv
                i3 = i2 * inv
                s1 = (screen - damp) * i3 + g * i2
                s2 = 3.0 * (screen - (1.0 + u3) * damp) * (i3 * i2) + g * (
                    2.0 * BETA * BETA + 3.0 * i2
                ) * i2
                s1 = jnp.where(itself, 0.0, s1)
                s2 = jnp.where(itself, 0.0, s2)
                ax, ay, az = s2 * dx, s2 * dy, s2 * dz
                xx, xy, xz = ax * dx - s1, ax * dy, ax * dz
                yy, yz, zz = ay * dy - s1, ay * dz, az * dz - s1
                for c, value in enumerate((xx, xy, xz, yy, yz, zz)):
                    coef[at, c, cut, :] = value
            else:
                dip = near1[entry]
                xx, xy, xz, yy, yz, zz = (coef[at, c, cut, :] for c in range(6))
            out = []
            for s in range(2):
                vx, vy, vz = (dip[3 * s + c : 3 * s + c + 1] for c in range(3))
                out.append(sums[3 * s] + (xx * vx + xy * vy + xz * vz))
                out.append(sums[3 * s + 1] + (xy * vx + yy * vy + yz * vz))
                out.append(sums[3 * s + 2] + (xz * vx + yz * vy + zz * vz))
            return tuple(out)

        zero = jnp.zeros((block, TILE), jnp.float32)
        sums = lax.fori_loop(0, NBR, body, (zero,) * 6)
        for c in range(6):
            acc[t, c, cut, :] = sums[c]

    units = TILES * blocks

    def pairs(op, begin, end):
        @pl.loop(begin, end)
        def _(unit):
            pair_unit(op, unit)

    def finish_pairs():
        direct[...] = jnp.zeros((8, ATOMS), jnp.float32)
        for t in range(TILES):
            for c in range(6):
                total = jnp.sum(acc[t, c].T, axis=0, keepdims=True)
                direct[c : c + 1, t * TILE : (t + 1) * TILE] = total

    def by_rhs(v, d):
        first = jnp.broadcast_to(v[d : d + 1], (8, ATOMS))
        second = jnp.broadcast_to(v[3 + d : 4 + d], (8, ATOMS))
        choice = (first, second, jnp.where(first_half, first, second))
        return jnp.concatenate([choice[s] for s in GROUP_S], axis=0)

    def fold_rows(product, s):
        total = None
        for g, kind in enumerate(GROUP_S):
            piece = product[8 * g : 8 * g + 8]
            if kind == 2:
                piece = jnp.where(first_half if s == 0 else ~first_half, piece, 0.0)
            elif kind != s:
                continue
            total = piece if total is None else total + piece
        return jnp.sum(total, axis=0, keepdims=True)

    def image(op, v):
        phase = 7 * op
        cuts = CHUNKS[op]
        flat = by_rhs(v, 0) * pdx[...] + by_rhs(v, 1) * pdy[...]
        steep = by_rhs(v, 2) * pdf[...]
        hsend[op] = mm(flat, zhat_t[0:ATOMS, :]) + mm(steep, zhat_t[ATOMS:, :])
        for dr, dc in NEIGHBOURS:
            first, count = CUTS[dr, dc]
            remote(
                hsend.at[op, pl.ds(first, count)], hrecv.at[op, pl.ds(first - CENTRE, count)],
                phase + 1, to(dr, dc),
            )
        if op == 1:
            send_near(dsend1, near1, phase)
        else:
            arrived(near0, 0)
        pairs(op, cuts[0], cuts[1])
        arrived(hrecv.at[op], phase + 1)
        whole = jnp.concatenate([hsend[op, 0:CENTRE, :], hrecv[op]], axis=0)
        lines = mm(whole[:, 0:128].T, mt[0]) + mm(whole[:, 128:256].T, mt[1])
        swapped = swap_bits(lines.reshape(COLS // 2, 8, LANES), 16)
        csend[op] = swapped.reshape(COLS, CY, LANES)

        @pl.loop(1, COLS)
        def _(k):
            c = lax.rem(me_c + k, COLS)
            remote(csend.at[op, c], crecv.at[op, me_c], phase + 2, (me_r, c))

        keep(csend.at[op, me_c], crecv.at[op, me_c], phase + 2)
        if op == 1:
            arrived(near1, phase)
        pairs(op, cuts[1], cuts[2])
        arrived(crecv.at[op], phase + 2)
        along_y = mm(hy[...], crecv[op].reshape(GY, LANES))
        rsend[op] = along_y.reshape(ROWS, 8, LANES)

        @pl.loop(1, ROWS)
        def _(k):
            r = lax.rem(me_r + k, ROWS)
            remote(rsend.at[op, r], rrecv.at[op, me_r], phase + 3, (r, me_c))

        keep(rsend.at[op, me_r], rrecv.at[op, me_r], phase + 3)
        pairs(op, cuts[2], cuts[3])
        arrived(rrecv.at[op], phase + 3)
        lines_x = swap_bits(rrecv[op], 1).reshape(GX, LANES)
        along_x = mm(hx[...], lines_x) * infl[...]
        back_x = mm(hx[...], along_x)
        ssend[op] = swap_bits(back_x.reshape(ROWS, 8, LANES), 1)

        @pl.loop(1, ROWS)
        def _(k):
            r = lax.rem(me_r + k, ROWS)
            remote(ssend.at[op, r], srecv.at[op, me_r], phase + 4, (r, me_c))

        keep(ssend.at[op, me_r], srecv.at[op, me_r], phase + 4)
        pairs(op, cuts[3], cuts[4])
        arrived(srecv.at[op], phase + 4)
        back_y = mm(hy[...], srecv[op].reshape(GY, LANES))
        tsend[op] = back_y.reshape(COLS, CY, LANES)

        @pl.loop(1, COLS)
        def _(k):
            c = lax.rem(me_c + k, COLS)
            remote(tsend.at[op, c], trecv.at[op, me_c], phase + 5, (me_r, c))

        keep(tsend.at[op, me_c], trecv.at[op, me_c], phase + 5)
        pairs(op, cuts[4], cuts[5])
        arrived(trecv.at[op], phase + 5)
        packed = swap_bits(trecv[op].reshape(COLS // 2, 8, LANES), 16).reshape(128, LANES)
        gsend[op, :, 0:128] = mm(mt[0], packed, ((1,), (1,)))
        gsend[op, :, 128:256] = mm(mt[1], packed, ((1,), (1,)))
        for dr, dc in NEIGHBOURS:
            first, count = CUTS[-dr, -dc]
            remote(
                gsend.at[op, pl.ds(first, count)], grecv.at[op, pl.ds(first - CENTRE, count)],
                phase + 6, to(dr, dc),
            )
        pairs(op, cuts[5], units)
        finish_pairs()
        arrived(grecv.at[op], phase + 6)
        whole = jnp.concatenate([gsend[op, 0:CENTRE, :], grecv[op]], axis=0)
        level = mm(whole, zhat[:, 0:ATOMS])
        steep = mm(whole, zhat[:, ATOMS:])
        parts = (level * pdx[...], level * pdy[...], steep * pdf[...])
        vec[...] = jnp.zeros((8, ATOMS), jnp.float32)
        for s in range(2):
            for d in range(3):
                vec[3 * s + d : 3 * s + d + 1, :] = fold_rows(parts[d], s)
        return v / alpha - direct[...] + vec[...] - SELF * v

    lane_row = lax.broadcasted_iota(jnp.int32, (1, LANES), 1)

    def inner(left_v, right_v, s):
        product = jnp.where((row_id >= 3 * s) & (row_id < 3 * s + 3), left_v * right_v, 0.0)
        return jnp.sum(jnp.sum(product, axis=0, keepdims=True), axis=1, keepdims=True)

    def pack(numbers):
        out = jnp.zeros((1, LANES), jnp.float32)
        for n, value in enumerate(numbers):
            out = jnp.where(lane_row == n, value, out)
        return out

    def unpack(line, n):
        return jnp.sum(jnp.where(lane_row == n, line, 0.0), axis=1, keepdims=True)

    def sum_cols(op, line):
        psend[op] = line

        @pl.loop(1, COLS)
        def _(k):
            c = lax.rem(me_c + k, COLS)
            remote(psend.at[op], pcol.at[op, me_c], 14 + 2 * op, (me_r, c))

        keep(psend.at[op], pcol.at[op, me_c], 14 + 2 * op)

    def sum_rows(op):
        arrived(pcol.at[op], 14 + 2 * op)
        psend2[op] = jnp.sum(pcol[op], axis=0)

        @pl.loop(1, ROWS)
        def _(k):
            r = lax.rem(me_r + k, ROWS)
            remote(psend2.at[op], prow.at[op, me_r], 15 + 2 * op, (r, me_c))

        keep(psend2.at[op], prow.at[op, me_r], 15 + 2 * op)

    def sum_done(op):
        arrived(prow.at[op], 15 + 2 * op)
        return jnp.sum(prow[op], axis=0)

    def wide(numbers):
        row = lax.broadcasted_iota(jnp.int32, (8, 1), 0)
        return jnp.where(row < 3, numbers[0], numbers[1])

    q1 = image(0, d1)
    w1 = alpha * q1
    for t in range(TILES):
        dsend1[t] = w1[:, t * TILE : (t + 1) * TILE]
    sum_cols(
        0,
        pack(
            [inner(r0, d1, 0), inner(r0, d1, 1), inner(d1, q1, 0), inner(d1, q1, 1), inner(q1, w1, 0), inner(q1, w1, 1)]
        ),
    )
    rowbuf[0] = q1
    rowbuf[1] = w1
    z1 = image(1, w1)
    sum_rows(0)
    line = sum_done(0)
    progress = [unpack(line, s) for s in range(2)]
    step = [progress[s] / unpack(line, 2 + s) for s in range(2)]
    following = [step[s] * step[s] * unpack(line, 4 + s) - progress[s] for s in range(2)]
    ratio = [following[s] / progress[s] for s in range(2)]
    step_w = wide(step)
    grown = 1.0 + wide(ratio)
    q1 = rowbuf[0]
    w1 = rowbuf[1]
    d2 = grown * d1 - step_w * w1
    q2 = grown * q1 - step_w * z1
    sum_cols(1, pack([inner(d2, q2, 0), inner(d2, q2, 1)]))
    x1 = step_w * d1
    r1 = r0 - step_w * q1
    sum_rows(1)
    line = sum_done(1)
    step2 = wide([following[s] / unpack(line, s) for s in range(2)])
    x2 = x1 + step2 * d2
    r2 = r1 - step2 * q2
    vec[...] = x2
    out_x[0, 0, 0] = vec[0:3, :]
    out_x[0, 0, 1] = vec[3:6, :]
    vec[...] = r2
    out_r[0, 0, 0] = vec[0:3, :]
    out_r[0, 0, 1] = vec[3:6, :]

    left(near0.at[pl.ds(0, 8 * TILES)], 0)
    left(near1.at[pl.ds(0, 8 * TILES)], 7)
    for op in range(2):
        left(hrecv.at[op], 7 * op + 1)
        left(crecv.at[op, pl.ds(0, COLS - 1)], 7 * op + 2)
        left(rrecv.at[op, pl.ds(0, ROWS - 1)], 7 * op + 3)
        left(srecv.at[op, pl.ds(0, ROWS - 1)], 7 * op + 4)
        left(trecv.at[op, pl.ds(0, COLS - 1)], 7 * op + 5)
        left(grecv.at[op], 7 * op + 6)
        left(pcol.at[op, pl.ds(0, COLS - 1)], 14 + 2 * op)
        left(prow.at[op, pl.ds(0, ROWS - 1)], 15 + 2 * op)


CHUNKS = ((0, 5, 10, 16, 21, 27), (0, 0, 7, 13, 19, 25))


def local(field, place, polar, base, lists):
    vmem = pl.BlockSpec(memory_space=pltpu.VMEM)
    smem = pl.BlockSpec(memory_space=pltpu.SMEM)
    f32 = jnp.float32

    def buf(*shape):
        return pltpu.VMEM(shape, f32)

    out = jax.ShapeDtypeStruct((1, 1, 2, 3, ATOMS), f32)
    return pl.pallas_call(
        kernel,
        out_shape=(out, out),
        in_specs=[vmem] * 4 + [smem] + [vmem] * 8,
        out_specs=(vmem, vmem),
        scratch_shapes=[
            buf(ALL, ATOMS), buf(ALL, ATOMS), buf(ALL, ATOMS),
            buf(KZ, 2 * ATOMS), buf(2 * ATOMS, KZ), buf(GX, LANES),
            buf(TILES, 4, TILE, TILE), buf(TILES * NBR, 6, TILE, TILE), buf(TILES, 6, TILE, TILE),
            buf(8, ATOMS), buf(8, ATOMS), buf(2, 8, ATOMS),
            buf(TILES, 16, TILE), buf(TILES, 8, TILE), buf(9 * TILES, 16, TILE), buf(9 * TILES, 8, TILE),
            buf(2, ALL, KZ), buf(2, OUTER, KZ),
            buf(2, COLS, CY, LANES), buf(2, COLS, CY, LANES),
            buf(2, ROWS, 8, LANES), buf(2, ROWS, 8, LANES),
            buf(2, ROWS, 8, LANES), buf(2, ROWS, 8, LANES),
            buf(2, COLS, CY, LANES), buf(2, COLS, CY, LANES),
            buf(2, ALL, KZ), buf(2, OUTER, KZ),
            buf(2, 1, LANES), buf(2, COLS, 1, LANES), buf(2, 1, LANES), buf(2, ROWS, 1, LANES),
            pltpu.SemaphoreType.DMA((18,)), pltpu.SemaphoreType.DMA((18,)),
        ],
        compiler_params=pltpu.CompilerParams(
            collective_id=0, has_side_effects=True, vmem_limit_bytes=56 * 1024 * 1024
        ),
    )(field, place, polar.reshape(1, 1, 1, ATOMS), base, lists, *(jnp.asarray(c) for c in constants()))


def solution(mesh):
    placed = (
        P("row", "col", None, None, None),
        P("row", "col", None, None),
        P("row", "col", None),
        P("row", "col", None, None),
        P("row", "col", None, None),
    )
    return jax.shard_map(
        local,
        mesh=mesh,
        in_specs=placed,
        out_specs=(P("row", "col", None, None, None), P("row", "col", None, None, None)),
        check_vma=False,
    )
```

time: 891 us -> 176 us (0.20); the launches traced: 879 us -> 176 us
  blocking collectives: 371 us -> 0 us
  starting transfers between devices: 209 us -> 0 us
  Pallas kernels: 0 us -> 171 us
  waiting for transfers between devices: 94.4 us -> 0 us
  other arithmetic: 92.1 us -> 0 us
  local copies, waits for them, and re-layouts: 77.2 us -> 4.45 us
  matrix products: 17.6 us -> 0 us
  loops' own time: 15.9 us -> 0 us
    psum x3 -> x0, blocking collectives: 324 us -> none  [inner_sum(): return lax.psum(jnp.sum(left_arr * right_arr, axis=(1, 2)), ('row', 'col'))]
    ppermute x28 -> x0, starting transfers between devices: 172 us -> none  [the longest x14 141 us: with_halo(): lax.ppermute(head, axis, [((i + 1) % count, i) for i in range(count)])]
    pallas_call x0 -> x1, Pallas kernels: none -> 171 us  [local(): pl.pallas_call(kernel, out_shape=(out, out), in_specs=[vmem] * 4 + [smem]...]
    ppermute x28 -> x0, waiting for transfers between devices: 54.6 us -> none  [the longest x14 54.6 us: with_halo(): lax.ppermute(tail, axis, [(i, (i + 1) % count) for i in range(count)])]
    all_to_all x2 -> x0, blocking collectives: 46.2 us -> none  [the longest x1 24.4 us: local(): lax.all_to_all(along_y, 'row', split_axis=2, concat_axis=1, tiled=True)]
    select_n x32 -> x0, other arithmetic: 40.6 us -> none  [the longest x8 20.7 us: tile_field(): second = jnp.where(itself, 0.0, second)]
    all_to_all x6 -> x0, waiting for transfers between devices: 39.8 us -> none  [the longest x1 16 us: local(): lax.all_to_all(spectrum, 'col', split_axis=3, concat_axis=2, tiled=True)]
    all_to_all x6 -> x0, starting transfers between devices: 36.2 us -> none  [the longest x1 15.7 us: local(): lax.all_to_all(along_y, 'row', split_axis=2, concat_axis=1, tiled=True)]
  transfers between devices with their start and end apart: 34 -> 0, of which waited for: 12 -> 0; matrix products, arithmetic and copies ran while one was open for 18% -> 0% of each run, Pallas kernels for 0% -> 0%
where the time goes in v1:
time: 176 us
  Pallas kernels  171 us (97%)
  local copies, waits for them, and re-layouts  4.45 us (3%)
    pallas_call x1, Pallas kernels, local(): pl.pallas_call(kernel, out_shape=(out, out), in_specs=[vmem] * 4 + [smem]...  171 us

profile of v1, /device:TPU:1, one launch (start us, length us, event | category | flops | bytes accessed | tf_op | source)
XLA Modules:
  0.0 176.2 jit_solution(14377842022635121274)
XLA Ops:
  0.6 0.0 copy-start.2
  0.6 0.0 copy-start.1
  0.6 1.3 copy.16.place
  2.0 0.0 copy-done.2
  2.0 0.6 copy.17.base
  2.6 0.0 copy-done.1
  2.6 0.6 copy.15.field
  3.2 171.1 %shard_map.140 = (f32[1,1,2,3,512]{4,3,2,1,0:T(4,128)}, f32[1,1,2,3,512]{4,3,2,1,0:T(4,128)}) custom-call(f32[1,1,2,3,512]{4,3,2,1,0:T(4,128)} %copy.15.field, f32[1,1,3,512]{3,2,1,0:T(4,128)} %copy.16.place, f32[1,1,1,512]{3,2,1,0:T(1,128)} %bitcast.1, s32[1,1,3,512]{3,2,1,0:T(4,128)} %copy.17.base, s32[1,1,4,12]{3,2,1,0:T(4,128)} %lists.1, ...), custom_call_target="tpu_custom_call" | custom-call | tf_op jit(solution)/shard_map/pallas_call | solution.py:579
  174.3 0.0 copy-start
  174.3 1.3 copy.18
  175.6 0.0 copy-done
  175.6 0.6 copy.19
Async XLA Ops:
  0.6 1.3 copy-start.2
  0.6 1.9 %copy-start.1 = (f32[1,1,2,3,512]{4,2,3,1,0:T(2,128)S(1)}, f32[1,1,2,3,512]{4,2,3,1,0:T(2,128)}, u32[]{:S(2)}) copy-start(f32[1,1,2,3,512]{4,2,3,1,0:T(2,128)} %param.13) | copy-start | bytes 36868
  174.3 1.3 copy-start

commit v2 on v1

v2 whole, which is shorter than its diff:
```python
import functools
import math

import jax
import jax.numpy as jnp
import numpy as np
from jax import lax
from jax.experimental import pallas as pl
from jax.experimental.pallas import tpu as pltpu
from jax.sharding import PartitionSpec as P

MESH = pl.DeviceIdType.MESH
CX = 8
CY = 4
KZ = 256
TILE = 128
TILES = 4
NBR = 12
ATOMS = TILE * TILES
ROWS = 16
COLS = 32
GX = CX * ROWS
GY = CY * COLS
LANES = 128

BETA = 0.4
THOLE = 0.39
SELF = 4.0 * BETA**3 / (3.0 * math.sqrt(math.pi))
ERFCX = (
    0.22567586600780487,
    0.2256697714328766,
    0.20783858001232147,
    0.16857817769050598,
    0.14127734303474426,
    -0.005255409982055426,
    0.16864386200904846,
    -0.18261533975601196,
    0.05018728971481323,
)

NEIGHBOURS = [(dr, dc) for dr in (-1, 0, 1) for dc in (-1, 0, 1) if (dr, dc) != (0, 0)]
ROW_STEP = {-1: ROWS - 1, 0: 0, 1: 1}
COL_STEP = {-1: COLS - 1, 0: 0, 1: 1}

PLANE = 16
LINE = 32
SLOTS = 24


def region_rows():
    rows = []
    for yh in range(2):
        for s in range(2):
            for j in range(6):
                rows += [(2 * j + e - 2, 4 * yh + yl - 2, s) for e in range(2) for yl in range(4)]
    return rows


REGION = region_rows()
ALL = len(REGION)
SLOT_ROW = [slot // 6 * 8 + slot % 6 for slot in range(SLOTS)]
SLOT_S = [slot // 6 % 2 for slot in range(SLOTS)]


def cas(rows, cols, length):
    angle = 2.0 * np.pi / length * ((rows[:, None] * cols[None, :]) % length)
    return (np.cos(angle) + np.sin(angle)).astype(np.float32)


def wave_tables(length):
    k = np.arange(length)
    f = np.minimum(k, length - k) / length
    c = np.array([1.0, 11.0, 11.0, 1.0]) / 24.0
    angle = 2.0 * np.pi / length * ((k[:, None] * np.arange(4)[None, :]) % length)
    b = (np.cos(angle) @ c) ** 2 + (np.sin(angle) @ c) ** 2
    inverse = np.where(2 * k == length, 0.0, 1.0 / np.where(2 * k == length, 1.0, b))
    return (f * f), inverse


def constants():
    q = np.arange(KZ)
    hz = cas(16 * (q % 16) + q // 16, np.arange(KZ), KZ)
    cells = np.zeros((2, ALL, LANES), np.int32)
    for row, (x, y, _) in enumerate(REGION):
        cells[0, row] = x
        cells[1, row] = y
    row = np.arange(128)
    device, line = row // 8, row % 8
    kx = np.arange(GX)
    stack = []
    for e in range(2):
        stack.append(cas(kx, 8 * device + 2 * line + e - 2, GX) * (line < 6))
    for e in range(2):
        for jq in range(3):
            stack.append(cas(kx, 8 * device + 2 * (2 * jq + line - 6) + e - 2, GX) * (line >= 6))
    hx = np.stack(stack).astype(np.float32)
    lane = np.arange(LANES)
    yb, group, yl = lane // 32, lane // 8 % 4, lane % 4
    ky = np.arange(GY)
    parts = [cas(32 * yb + 16 * zh + 4 * group + yl - 2, ky, GY) for zh in range(2)]
    parts += [cas(32 * yb + 16 * zh + 16 + yl - 2, ky, GY) * (group < 3)[:, None] for zh in range(2)]
    hy = np.concatenate(parts, axis=0).astype(np.float32)
    fx, bx = wave_tables(GX)
    fy, by = wave_tables(GY)
    fz, bz = wave_tables(KZ)
    scale = 1.0 / (GX * GY * KZ * math.pi)
    fx_rows = np.broadcast_to(np.stack([fx, bx * scale])[:, :, None], (2, GX, LANES)).astype(np.float32)
    fy_rows = np.stack([fy, by])[:, None, :].astype(np.float32)
    wave = 16 * np.arange(PLANE)[:, None] + (lane // 8)[None, :]
    fz_rows = np.stack([fz[wave], bz[wave]]).astype(np.float32)
    return hz, hx, hx.transpose(0, 2, 1).copy(), hy, hy.T.copy(), cells, fx_rows, fy_rows, fz_rows


def mm(a, b, dims=((1,), (0,))):
    return lax.dot_general(
        a, b, (dims, ((), ())), precision=lax.Precision.HIGHEST, preferred_element_type=jnp.float32
    )


def swap_blocks(tiles):
    tiles = list(tiles)
    block = lax.broadcasted_iota(jnp.int32, tiles[0].shape, 1) // 8
    for bit in (1, 2, 4, 8):
        low = block & bit == 0
        for n in range(16):
            if n & bit == 0:
                one, two = tiles[n], tiles[n | bit]
                tiles[n] = jnp.where(low, one, pltpu.roll(two, 8 * bit, 1))
                tiles[n | bit] = jnp.where(low, pltpu.roll(one, LANES - 8 * bit, 1), two)
    return tiles


def spline(fraction):
    previous = {0: jnp.ones_like(fraction)}
    fourth = previous
    for degree in range(2, 6):
        current = {}
        for offset in range(degree):
            abscissa = fraction + float(offset)
            summed = (float(degree) - abscissa) * previous[offset - 1] if offset else None
            if offset in previous:
                term = abscissa * previous[offset]
                summed = term if summed is None else term + summed
            current[offset] = summed * (1.0 / (degree - 1))
        if degree == 4:
            fourth = current
        previous = current
    values = [previous[4 - j] for j in range(5)]
    slopes = []
    for j in range(5):
        low = fourth.get(4 - j)
        high = fourth.get(3 - j)
        slopes.append(-high if low is None else low if high is None else low - high)
    return values, slopes


def kernel(
    field, place, polar, base, lists, hz, hx, hx_t, hy, hy_t, cells, fx, fy, fz,
    out_x, out_r,
    pdx, pdy, pdf, zhat, zhat_t, infl, own, coef, acc, direct, vec, keepv, spectrum,
    dsend0, dsend1, near0, near1, asend, arecv, bsend, brecv, csend, crecv, esend, erecv,
    psend, pplane, psend2, pline,
    send_sem, recv_sem,
):
    me_r = lax.axis_index("row")
    me_c = lax.axis_index("col")
    me_x = lax.rem(me_c, 4)
    me_y = me_c // 8
    me_h = lax.rem(me_c // 4, 2)
    me_a = me_y * 4 + me_x
    me_b = me_h * 16 + me_r

    def to(dr, dc):
        return (lax.rem(me_r + ROW_STEP[dr], ROWS), lax.rem(me_c + COL_STEP[dc], COLS))

    def plane_device(a):
        return (me_r, a // 4 * 8 + me_h * 4 + lax.rem(a, 4))

    def line_device(b):
        return (lax.rem(b, 16), me_y * 8 + b // 16 * 4 + me_x)

    def each_plane(body):
        @pl.loop(1, PLANE)
        def _(k):
            a = lax.rem(me_a + k, PLANE)
            body(a, plane_device(a))

    def each_line(body):
        @pl.loop(1, LINE)
        def _(k):
            step = k // 2
            off = 16 + step * (1 - 2 * lax.rem(k, 2))
            b = lax.rem(me_b + off + LINE, LINE)
            body(b, line_device(b))

    barrier = pltpu.get_barrier_semaphore()

    def greet(_, device):
        pl.semaphore_signal(barrier, 1, device_id=device, device_id_type=MESH)

    each_line(greet)
    each_plane(greet)
    for dr, dc in NEIGHBOURS:
        if dc:
            greet(None, to(dr, dc))

    def remote(src, dst, phase, device):
        pltpu.make_async_remote_copy(
            src_ref=src, dst_ref=dst, send_sem=send_sem.at[phase], recv_sem=recv_sem.at[phase],
            device_id=device, device_id_type=MESH,
        ).start()

    def keep(src, dst, phase):
        pltpu.make_async_copy(src, dst, recv_sem.at[phase]).start()

    def arrived(ref, phase):
        pltpu.make_async_copy(ref, ref, recv_sem.at[phase]).wait()

    def left(ref, phase):
        pltpu.make_async_copy(ref, ref, send_sem.at[phase]).wait()

    def rows6(ref):
        vec[...] = jnp.zeros((8, ATOMS), jnp.float32)
        vec[0:3, :] = ref[0, 0, 0]
        vec[3:6, :] = ref[0, 0, 1]
        return vec[...]

    row_id = lax.broadcasted_iota(jnp.int32, (8, ATOMS), 0)
    alpha = polar[0, 0:1, 0, :]
    r0 = rows6(field)
    d1 = alpha * r0

    iroot = jnp.exp(jnp.log(alpha) * (-1.0 / 6.0))
    vec[0:3, :] = place[0, 0]
    vec[3:4, :] = iroot
    vec[4:8, :] = jnp.zeros((4, ATOMS), jnp.float32)
    for t in range(TILES):
        cut = slice(t * TILE, (t + 1) * TILE)
        dsend0[t, 0:8, :] = vec[:, cut]
        dsend0[t, 8:16, :] = d1[:, cut]
    vec[0:3, :] = place[0, 0]
    vec[3:8, :] = jnp.zeros((5, ATOMS), jnp.float32)
    cell = base[0, 0] + 2
    axis_row = lax.broadcasted_iota(jnp.int32, (3, ATOMS), 0)
    cell = cell & jnp.where(axis_row == 2, KZ - 1, GX - 1)
    fraction = place[0, 0] - cell.astype(jnp.float32)
    values, slopes = spline(fraction)
    base_all = base[0, 0]
    rel_x = ((base_all[0:1] - me_r * CX + 2) & (GX - 1)) - 2
    rel_y = ((base_all[1:2] - me_c * CY + 2) & (GY - 1)) - 2
    rel_z = base_all[2:3]

    def placed(step, row):
        value = jnp.zeros(step.shape, jnp.float32)
        slope = jnp.zeros(step.shape, jnp.float32)
        for j in range(5):
            here = step == j
            value = jnp.where(here, values[j][row : row + 1], value)
            slope = jnp.where(here, slopes[j][row : row + 1], slope)
        return value, slope

    for g in range(ALL // 32):
        cut = slice(32 * g, 32 * g + 32)
        cell_x = jnp.concatenate([cells[0, cut, :]] * TILES, axis=1)
        cell_y = jnp.concatenate([cells[1, cut, :]] * TILES, axis=1)
        tx, sx = placed(cell_x - rel_x, 0)
        ty, sy = placed(cell_y - rel_y, 1)
        pdx[cut, :] = sx * ty
        pdy[cut, :] = tx * sy
        pdf[cut, :] = tx * ty
    step_z = (lax.broadcasted_iota(jnp.int32, (KZ, ATOMS), 0) - rel_z) & (KZ - 1)
    tz, sz = placed(step_z, 2)
    zhat[:, 0:ATOMS] = mm(hz[...], tz)
    zhat[:, ATOMS:] = mm(hz[...], sz)
    zhat_t[...] = zhat[...].T

    lane_row = lax.broadcasted_iota(jnp.int32, (1, LANES), 1)
    mine = lane_row == 8 * lax.rem(me_b, 16)
    row_z = fz[:, pl.ds(me_a, 1), :]
    f_z = jnp.sum(jnp.where(mine, row_z[0], 0.0), axis=1, keepdims=True)
    b_z = jnp.sum(jnp.where(mine, row_z[1], 0.0), axis=1, keepdims=True)
    m2 = fx[0] + (fy[0] + f_z)
    zero = m2 == 0.0
    safe = jnp.where(zero, 1.0, m2)
    shape = jnp.exp(-(math.pi**2 / BETA**2) * safe) / safe * (fx[1] * (fy[1] * b_z))
    infl[...] = jnp.where(zero, 0.0, shape)

    for t in range(TILES):
        cut = slice(t * TILE, (t + 1) * TILE)
        for c in range(4):
            source = iroot[:, cut] if c == 3 else place[0, 0, c : c + 1, cut]
            own[t, c] = jnp.broadcast_to(source, (TILE, TILE)).T

    for op in range(2):
        asend[op] = jnp.zeros((PLANE * 32, LANES), jnp.float32)

    def send_near(src, dst, phase):
        for dr, dc in NEIGHBOURS:
            slot = (1 - dr) * 3 + (1 - dc)
            remote(src, dst.at[pl.ds(slot * TILES, TILES)], phase, to(dr, dc))
        keep(src, dst.at[pl.ds(4 * TILES, TILES)], phase)

    def pair_unit(op, unit):
        block = PAIR_BLOCK[op]
        blocks = TILE // block
        t = unit // blocks
        first = pl.multiple_of((unit - t * blocks) * block, block)
        cut = pl.ds(first, block)
        lane = lax.broadcasted_iota(jnp.int32, (block, TILE), 1)
        line = lax.broadcasted_iota(jnp.int32, (block, TILE), 0) + first

        def body(k, sums):
            entry = lists[0, 0, t, k]
            at = t * NBR + k
            if op == 0:
                near = near0[entry]
                dip = near[8:16]
                delta = []
                for c, span in ((0, GX), (1, GY), (2, KZ)):
                    d = near[c : c + 1] - own[t, c, cut, :]
                    delta.append(d - float(span) * jnp.floor(d * (1.0 / span) + 0.5))
                dx, dy, dz = delta
                sq = dx * dx + dy * dy + dz * dz
                itself = line + k * TILE == lane
                sq = jnp.where(itself, 1.0, sq)
                inv = lax.rsqrt(sq)
                rho = sq * inv
                scaled = rho * (own[t, 3, cut, :] * near[3:4])
                u3 = THOLE * (scaled * scaled * scaled)
                damp = jnp.exp(-u3)
                gauss = jnp.exp(-(BETA * BETA) * sq)
                t_ = 1.0 / (1.0 + (0.4 * BETA) * rho)
                poly = jnp.full_like(t_, ERFCX[-1])
                for c in ERFCX[-2::-1]:
                    poly = poly * t_ + c
                screen = gauss * (t_ * poly)
                g = (2.0 * BETA / math.sqrt(math.pi)) * gauss
                i2 = inv * inv
                i3 = i2 * inv
                s1 = (screen - damp) * i3 + g * i2
                s2 = 3.0 * (screen - (1.0 + u3) * damp) * (i3 * i2) + g * (
                    2.0 * BETA * BETA + 3.0 * i2
                ) * i2
                s1 = jnp.where(itself, 0.0, s1)
                s2 = jnp.where(itself, 0.0, s2)
                ax, ay, az = s2 * dx, s2 * dy, s2 * dz
                xx, xy, xz = ax * dx - s1, ax * dy, ax * dz
                yy, yz, zz = ay * dy - s1, ay * dz, az * dz - s1
                for c, value in enumerate((xx, xy, xz, yy, yz, zz)):
                    coef[at, c, cut, :] = value
            else:
                dip = near1[entry]
                xx, xy, xz, yy, yz, zz = (coef[at, c, cut, :] for c in range(6))
            out = []
            for s in range(2):
                vx, vy, vz = (dip[3 * s + c : 3 * s + c + 1] for c in range(3))
                out.append(sums[3 * s] + (xx * vx + xy * vy + xz * vz))
                out.append(sums[3 * s + 1] + (xy * vx + yy * vy + yz * vz))
                out.append(sums[3 * s + 2] + (xz * vx + yz * vy + zz * vz))
            return tuple(out)

        zero = jnp.zeros((block, TILE), jnp.float32)
        sums = lax.fori_loop(0, NBR, body, (zero,) * 6)
        for c in range(6):
            acc[t, c, cut, :] = sums[c]

    def pairs(op, begin, end):
        @pl.loop(begin, end)
        def _(unit):
            pair_unit(op, unit)

    def finish_pairs():
        direct[...] = jnp.zeros((8, ATOMS), jnp.float32)
        for t in range(TILES):
            for c in range(6):
                total = jnp.sum(acc[t, c].T, axis=0, keepdims=True)
                direct[c : c + 1, t * TILE : (t + 1) * TILE] = total

    def by_rhs(v, d):
        choice = [jnp.broadcast_to(v[3 * s + d : 3 * s + d + 1], (8, ATOMS)) for s in range(2)]
        return jnp.concatenate([choice[s] for s in SLOT_S], axis=0)

    def fold_rows(product, s):
        total = None
        for slot, kind in enumerate(SLOT_S):
            if kind == s:
                piece = product[8 * slot : 8 * slot + 8]
                total = piece if total is None else total + piece
        return jnp.sum(total, axis=0, keepdims=True)

    def inner(left_v, right_v, s):
        product = jnp.where((row_id >= 3 * s) & (row_id < 3 * s + 3), left_v * right_v, 0.0)
        return jnp.sum(jnp.sum(product, axis=0, keepdims=True), axis=1, keepdims=True)

    def pack(numbers):
        out = jnp.zeros((1, LANES), jnp.float32)
        for n, value in enumerate(numbers):
            out = jnp.where(lane_row == n, value, out)
        return out

    def unpack(line, n):
        return jnp.sum(jnp.where(lane_row == n, line, 0.0), axis=1, keepdims=True)

    def sum_planes(op, line):
        psend[op] = line
        phase = 10 + 2 * op
        each_plane(lambda a, device: remote(psend.at[op], pplane.at[op, me_a], phase, device))
        keep(psend.at[op], pplane.at[op, me_a], phase)

    def sum_lines(op):
        arrived(pplane.at[op], 10 + 2 * op)
        psend2[op] = jnp.sum(pplane[op], axis=0)
        phase = 11 + 2 * op
        each_line(lambda b, device: remote(psend2.at[op], pline.at[op, me_b], phase, device))
        keep(psend2.at[op], pline.at[op, me_b], phase)

    def sum_done(op):
        arrived(pline.at[op], 11 + 2 * op)
        return jnp.sum(pline[op], axis=0)

    lane_wide = lax.broadcasted_iota(jnp.int32, (GX, 2 * LANES), 1)
    x_bit = lane_wide // 4 & 1 == 0
    group = lane_wide // 8 & 3

    def spread(op, v):
        phase = 5 * op
        flat = by_rhs(v, 0) * pdx[...] + by_rhs(v, 1) * pdy[...]
        steep = by_rhs(v, 2) * pdf[...]
        charge = mm(flat, zhat_t[0:ATOMS, :]) + mm(steep, zhat_t[ATOMS:, :])
        waves = jnp.concatenate([charge, jnp.zeros((KZ - ALL, KZ), jnp.float32)], axis=0).T
        tiles = []
        for i in range(16):
            piece = waves[16 * i : 16 * i + 16]
            tiles.append(jnp.concatenate([piece[:, 0:LANES], piece[:, LANES:]], axis=0))
        tiles = swap_blocks(tiles)
        for slot in range(SLOTS):
            part = tiles[slot % 16][slot // 16 * 16 : slot // 16 * 16 + 16]
            asend[op, pl.ds(SLOT_ROW[slot], 16, stride=32), :] = part
        mine = arecv.at[op, pl.ds(me_a * 32, 32)]
        each_plane(lambda a, device: remote(asend.at[op, pl.ds(a * 32, 32)], mine, phase + 1, device))
        keep(asend.at[op, pl.ds(me_a * 32, 32)], mine, phase + 1)

    def gather_planes(op):
        phase = 5 * op
        arrived(arecv.at[op], phase + 1)

        def got(a, yh):
            return jnp.concatenate(
                [arecv[op, a * 32 + (2 * yh + s) * 8 : a * 32 + (2 * yh + s) * 8 + 8, :] for s in range(2)], axis=0
            )

        row = lax.broadcasted_iota(jnp.int32, (16, LANES), 0) & 7
        tiles = []
        for yb in range(4):
            last = got(4 * yb + 3, 1)
            last = last.reshape(2, 8, LANES)
            for g in range(4):
                tile = got(4 * yb + g, 0)
                if g:
                    tile = tile + got(4 * yb + g - 1, 1)
                edge = 0.0
                if g < 3:
                    edge = pltpu.roll(last, 6 - 2 * g, 1).reshape(16, LANES)
                tiles.append(jnp.where(row < 6, tile, edge))
        tiles = swap_blocks(tiles)
        for i in range(16):
            bsend[op, i] = tiles[i][0:8]
            bsend[op, 16 + i] = tiles[i][8:16]
        each_line(lambda b, device: remote(bsend.at[op, b], brecv.at[op, me_b], phase + 2, device))
        keep(bsend.at[op, me_b], brecv.at[op, me_b], phase + 2)

    def convolve(op):
        phase = 5 * op
        arrived(brecv.at[op], phase + 2)
        lines = jnp.concatenate(
            [brecv[op, 0:16].reshape(GX, LANES), brecv[op, 16:32].reshape(GX, LANES)], axis=1
        )
        part = [mm(hx[n], lines) for n in range(8)]
        body = jnp.where(x_bit, part[0], part[1])
        edge = jnp.zeros_like(body)
        for jq in range(3):
            edge = jnp.where(group == jq, jnp.where(x_bit, part[2 + jq], part[5 + jq]), edge)
        waves = mm(jnp.concatenate([body, edge], axis=1), hy[...])
        spectrum[op] = waves
        back = mm(infl[...] * waves, hy_t[...])
        body, edge = back[:, 0 : 2 * LANES], back[:, 2 * LANES :]
        out = jnp.where(x_bit, mm(hx_t[0], body), mm(hx_t[1], body))
        for jq in range(3):
            piece = jnp.where(x_bit, mm(hx_t[2 + jq], edge), mm(hx_t[5 + jq], edge))
            out = out + jnp.where(group == jq, piece, 0.0)
        csend[op, 0:16] = out[:, 0:LANES].reshape(16, 8, LANES)
        csend[op, 16:32] = out[:, LANES:].reshape(16, 8, LANES)
        each_line(lambda b, device: remote(csend.at[op, b], crecv.at[op, me_b], phase + 3, device))
        keep(csend.at[op, me_b], crecv.at[op, me_b], phase + 3)

    def scatter_planes(op):
        phase = 5 * op
        arrived(crecv.at[op], phase + 3)
        tiles = swap_blocks([jnp.concatenate([crecv[op, i], crecv[op, 16 + i]], axis=0) for i in range(16)])
        row = lax.broadcasted_iota(jnp.int32, (16, LANES), 0) & 7
        for yb in range(4):
            edges = [
                pltpu.roll(tiles[4 * yb + g].reshape(2, 8, LANES), 2 + 2 * g, 1).reshape(16, LANES)
                for g in range(3)
            ]
            edge = jnp.where(row < 2, edges[0], jnp.where(row < 4, edges[1], edges[2]))
            for x in range(4):
                at = (4 * yb + x) * 32
                upper = tiles[4 * yb + x + 1] if x < 3 else edge
                esend[op, at : at + 16, :] = tiles[4 * yb + x]
                esend[op, at + 16 : at + 32, :] = upper
        mine = erecv.at[op, pl.ds(me_a * 32, 32)]
        each_plane(lambda a, device: remote(esend.at[op, pl.ds(a * 32, 32)], mine, phase + 4, device))
        keep(esend.at[op, pl.ds(me_a * 32, 32)], mine, phase + 4)

    def sample(op):
        phase = 5 * op
        arrived(erecv.at[op], phase + 4)
        none = jnp.zeros((16, LANES), jnp.float32)
        tiles = []
        for slot in range(16):
            one = erecv[op, pl.ds(SLOT_ROW[slot], 16, stride=32), :]
            two = erecv[op, pl.ds(SLOT_ROW[slot + 16], 16, stride=32), :] if slot < 8 else none
            tiles.append(jnp.concatenate([one, two], axis=0))
        tiles = swap_blocks(tiles)
        waves = jnp.concatenate(
            [jnp.concatenate([tile[0:16], tile[16:32]], axis=1) for tile in tiles], axis=0
        )
        whole = waves.T[0:ALL]
        level = mm(whole, zhat[:, 0:ATOMS])
        steep = mm(whole, zhat[:, ATOMS:])
        parts = (level * pdx[...], level * pdy[...], steep * pdf[...])
        vec[...] = jnp.zeros((8, ATOMS), jnp.float32)
        for s in range(2):
            for d in range(3):
                vec[3 * s + d : 3 * s + d + 1, :] = fold_rows(parts[d], s)
        return vec[...]

    def wide(numbers):
        row = lax.broadcasted_iota(jnp.int32, (8, 1), 0)
        return jnp.where(row < 3, numbers[0], numbers[1])

    def near_part(v):
        return v / alpha - SELF * v

    chunk = CHUNKS[0]
    units = TILES * TILE // PAIR_BLOCK[0]
    pl.semaphore_wait(barrier, PLANE - 1 + LINE - 1 + 6)
    spread(0, d1)
    send_near(dsend0, near0, 0)
    gather_planes(0)
    arrived(near0, 0)
    pairs(0, 0, chunk[0])
    convolve(0)
    pairs(0, chunk[0], chunk[1])
    scatter_planes(0)
    pairs(0, chunk[1], units)
    finish_pairs()
    recip = sample(0)
    direct1 = direct[...]
    q1 = near_part(d1) - direct1 + recip
    w1 = alpha * q1
    keepv[0] = direct1
    keepv[1] = q1
    keepv[2] = w1

    chunk = CHUNKS[1]
    units = TILES * TILE // PAIR_BLOCK[1]
    for t in range(TILES):
        dsend1[t] = w1[:, t * TILE : (t + 1) * TILE]
    spread(1, w1)
    send_near(dsend1, near1, 5)
    products = [inner(u, v, s) for u, v in ((r0, d1), (d1, q1), (q1, w1)) for s in range(2)]
    sum_planes(0, pack(products))
    gather_planes(1)
    sum_lines(0)
    arrived(near1, 5)
    pairs(1, 0, chunk[0])
    convolve(1)
    line = sum_done(0)
    progress = [unpack(line, s) for s in range(2)]
    step = [progress[s] / unpack(line, 2 + s) for s in range(2)]
    following = [step[s] * step[s] * unpack(line, 4 + s) - progress[s] for s in range(2)]
    ratio = [following[s] / progress[s] for s in range(2)]
    step_w = wide(step)
    grown = 1.0 + wide(ratio)
    pairs(1, chunk[0], units)
    finish_pairs()
    direct2 = grown * keepv[0] - step_w * direct[...]
    d2 = grown * d1 - step_w * keepv[2]
    local_part = near_part(d2) - direct2
    here = me_h == 0
    waves = jnp.where(here, 1.0 + ratio[0], 1.0 + ratio[1]) * spectrum[0]
    waves = waves - jnp.where(here, step[0], step[1]) * spectrum[1]
    power = jnp.sum(jnp.sum(infl[...] * (waves * waves), axis=0, keepdims=True), axis=1, keepdims=True)
    products = [inner(d2, local_part, s) for s in range(2)]
    sum_planes(1, pack(products) + jnp.where(lane_row == me_h, power, 0.0))
    scatter_planes(1)
    sum_lines(1)
    w1 = keepv[2]
    z1 = near_part(w1) - direct[...] + sample(1)
    q1 = keepv[1]
    d2 = grown * d1 - step_w * w1
    q2 = grown * q1 - step_w * z1
    x1 = step_w * d1
    r1 = r0 - step_w * q1
    line = sum_done(1)
    step2 = wide([following[s] / unpack(line, s) for s in range(2)])
    x2 = x1 + step2 * d2
    r2 = r1 - step2 * q2
    vec[...] = x2
    out_x[0, 0, 0] = vec[0:3, :]
    out_x[0, 0, 1] = vec[3:6, :]
    vec[...] = r2
    out_r[0, 0, 0] = vec[0:3, :]
    out_r[0, 0, 1] = vec[3:6, :]

    left(near0.at[pl.ds(0, 8 * TILES)], 0)
    left(near1.at[pl.ds(0, 8 * TILES)], 5)
    for op in range(2):
        left(arecv.at[op, pl.ds(0, 15 * 32)], 5 * op + 1)
        left(brecv.at[op, pl.ds(0, LINE - 1)], 5 * op + 2)
        left(crecv.at[op, pl.ds(0, LINE - 1)], 5 * op + 3)
        left(erecv.at[op, pl.ds(0, 15 * 32)], 5 * op + 4)
        left(pplane.at[op, pl.ds(0, PLANE - 1)], 10 + 2 * op)
        left(pline.at[op, pl.ds(0, LINE - 1)], 11 + 2 * op)


PAIR_BLOCK = (16, 32)
CHUNKS = ((10, 21), (6,))


def local(field, place, polar, base, lists):
    vmem = pl.BlockSpec(memory_space=pltpu.VMEM)
    smem = pl.BlockSpec(memory_space=pltpu.SMEM)
    f32 = jnp.float32

    def buf(*shape):
        return pltpu.VMEM(shape, f32)

    out = jax.ShapeDtypeStruct((1, 1, 2, 3, ATOMS), f32)
    return pl.pallas_call(
        kernel,
        out_shape=(out, out),
        in_specs=[vmem] * 4 + [smem] + [vmem] * 9,
        out_specs=(vmem, vmem),
        scratch_shapes=[
            buf(ALL, ATOMS), buf(ALL, ATOMS), buf(ALL, ATOMS),
            buf(KZ, 2 * ATOMS), buf(2 * ATOMS, KZ), buf(GX, LANES),
            buf(TILES, 4, TILE, TILE), buf(TILES * NBR, 6, TILE, TILE), buf(TILES, 6, TILE, TILE),
            buf(8, ATOMS), buf(8, ATOMS), buf(3, 8, ATOMS), buf(2, GX, GY),
            buf(TILES, 16, TILE), buf(TILES, 8, TILE), buf(9 * TILES, 16, TILE), buf(9 * TILES, 8, TILE),
            buf(2, PLANE * 32, LANES), buf(2, PLANE * 32, LANES),
            buf(2, LINE, 8, LANES), buf(2, LINE, 8, LANES), buf(2, LINE, 8, LANES), buf(2, LINE, 8, LANES),
            buf(2, PLANE * 32, LANES), buf(2, PLANE * 32, LANES),
            buf(2, 1, LANES), buf(2, PLANE, 1, LANES), buf(2, 1, LANES), buf(2, LINE, 1, LANES),
            pltpu.SemaphoreType.DMA((14,)), pltpu.SemaphoreType.DMA((14,)),
        ],
        compiler_params=pltpu.CompilerParams(
            collective_id=0, has_side_effects=True, vmem_limit_bytes=56 * 1024 * 1024
        ),
    )(field, place, polar.reshape(1, 1, 1, ATOMS), base, lists, *(jnp.asarray(c) for c in constants()))


def solution(mesh):
    placed = (
        P("row", "col", None, None, None),
        P("row", "col", None, None),
        P("row", "col", None),
        P("row", "col", None, None),
        P("row", "col", None, None),
    )
    return jax.shard_map(
        local,
        mesh=mesh,
        in_specs=placed,
        out_specs=(P("row", "col", None, None, None), P("row", "col", None, None, None)),
        check_vma=False,
    )
```

time: 176 us -> 122 us (0.69)
  Pallas kernels: 171 us -> 117 us
    pallas_call x1, Pallas kernels: 171 us -> 117 us  [local(): pl.pallas_call(kernel, out_shape=(out, out), in_specs=[vmem] * 4 + [smem]...]
where the time goes in v2:
time: 122 us
  Pallas kernels  117 us (96%)
  local copies, waits for them, and re-layouts  4.45 us (4%)
    pallas_call x1, Pallas kernels, local(): pl.pallas_call(kernel, out_shape=(out, out), in_specs=[vmem] * 4 + [smem]...  117 us
    unnamed x9, local copies, waits for them, and re-layouts  2.52 us

profile of v2, /device:TPU:1, one launch (start us, length us, event | category | flops | bytes accessed | tf_op | source)
XLA Modules:
  0.0 121.7 jit_solution(2165700629577185122)
XLA Ops:
  0.6 0.0 copy-start.2
  0.6 0.0 copy-start.1
  0.6 1.3 %copy.17.place = f32[1,1,3,512]{3,2,1,0:T(4,128)} copy(f32[1,1,3,512]{3,1,2,0:T(1,128)} %param.15) | data formatting | bytes 12288 | tf_op args[1]
  2.0 0.0 copy-done.2
  2.0 0.6 copy.18.base
  2.6 0.0 copy-done.1
  2.6 0.6 copy.16.field
  3.2 116.6 %shard_map.149 = (f32[1,1,2,3,512]{4,3,2,1,0:T(4,128)}, f32[1,1,2,3,512]{4,3,2,1,0:T(4,128)}) custom-call(f32[1,1,2,3,512]{4,3,2,1,0:T(4,128)} %copy.16.field, f32[1,1,3,512]{3,2,1,0:T(4,128)} %copy.17.place, f32[1,1,1,512]{3,2,1,0:T(1,128)} %bitcast.1, s32[1,1,3,512]{3,2,1,0:T(4,128)} %copy.18.base, s32[1,1,4,12]{3,2,1,0:T(4,128)} %lists.1, ...), custom_call_target="tpu_custom_call" | custom-call | tf_op jit(solution)/shard_map/pallas_call | solution.py:642
  119.8 0.0 copy-start
  119.8 1.3 %copy.19 = f32[1,1,2,3,512]{4,2,3,1,0:T(2,128)} copy(f32[1,1,2,3,512]{4,3,2,1,0:T(4,128)} %get-tuple-element.2) | data formatting | bytes 24576 | tf_op jit(solution)/shard_map/pallas_call | solution.py:642
  121.1 0.0 copy-done
  121.1 0.6 copy.20
Async XLA Ops:
  0.6 1.3 %copy-start.2 = (s32[1,1,3,512]{3,1,2,0:T(1,128)S(1)}, s32[1,1,3,512]{3,1,2,0:T(1,128)}, u32[]{:S(2)}) copy-start(s32[1,1,3,512]{3,1,2,0:T(1,128)} %param.17) | copy-start | bytes 18436
  0.6 1.9 %copy-start.1 = (f32[1,1,2,3,512]{4,2,3,1,0:T(2,128)S(1)}, f32[1,1,2,3,512]{4,2,3,1,0:T(2,128)}, u32[]{:S(2)}) copy-start(f32[1,1,2,3,512]{4,2,3,1,0:T(2,128)} %param.14) | copy-start | bytes 36868
  119.8 1.3 %copy-start = (f32[1,1,2,3,512]{4,3,2,1,0:T(4,128)S(1)}, f32[1,1,2,3,512]{4,3,2,1,0:T(4,128)}, u32[]{:S(2)}) copy-start(f32[1,1,2,3,512]{4,3,2,1,0:T(4,128)} %get-tuple-element.3) | copy-start | bytes 36868

commit v3 on v2

v3 whole, which is shorter than its diff:
```python
import functools
import math

import jax
import jax.numpy as jnp
import numpy as np
from jax import lax
from jax.experimental import pallas as pl
from jax.experimental.pallas import tpu as pltpu
from jax.sharding import PartitionSpec as P

MESH = pl.DeviceIdType.MESH
CX = 8
CY = 4
KZ = 256
TILE = 128
TILES = 4
NBR = 12
ATOMS = TILE * TILES
ROWS = 16
COLS = 32
GX = CX * ROWS
GY = CY * COLS
LANES = 128

BETA = 0.4
THOLE = 0.39
SELF = 4.0 * BETA**3 / (3.0 * math.sqrt(math.pi))
ERFCX = (
    0.22567586600780487,
    0.2256697714328766,
    0.20783858001232147,
    0.16857817769050598,
    0.14127734303474426,
    -0.005255409982055426,
    0.16864386200904846,
    -0.18261533975601196,
    0.05018728971481323,
)

NEIGHBOURS = [(dr, dc) for dr in (-1, 0, 1) for dc in (-1, 0, 1) if (dr, dc) != (0, 0)]
ROW_STEP = {-1: ROWS - 1, 0: 0, 1: 1}
COL_STEP = {-1: COLS - 1, 0: 0, 1: 1}

PLANE = 32
LINE = 16
SLOTS = 12


def region_rows():
    rows = []
    for yh in range(2):
        for j in range(6):
            for _ in range(2):
                rows += [(2 * j + e - 2, 4 * yh + yl - 2) for e in range(2) for yl in range(4)]
    return rows


REGION = region_rows()
ALL = len(REGION)
SLOT_ROW = [slot // 6 * 8 + slot % 6 for slot in range(SLOTS)]


def cas(rows, cols, length):
    angle = 2.0 * np.pi / length * ((rows[:, None] * cols[None, :]) % length)
    return (np.cos(angle) + np.sin(angle)).astype(np.float32)


def wave_tables(length):
    k = np.arange(length)
    f = np.minimum(k, length - k) / length
    c = np.array([1.0, 11.0, 11.0, 1.0]) / 24.0
    angle = 2.0 * np.pi / length * ((k[:, None] * np.arange(4)[None, :]) % length)
    b = (np.cos(angle) @ c) ** 2 + (np.sin(angle) @ c) ** 2
    inverse = np.where(2 * k == length, 0.0, 1.0 / np.where(2 * k == length, 1.0, b))
    return (f * f), inverse


def constants():
    q = np.arange(KZ)
    hz = cas(8 * (q % PLANE) + q // PLANE, np.arange(KZ), KZ)
    cells = np.zeros((2, ALL, LANES), np.int32)
    for row, (x, y) in enumerate(REGION):
        cells[0, row] = x
        cells[1, row] = y
    row = np.arange(128)
    chip, line = row // 16, row % 16
    kx = np.arange(GX)
    stack = []
    for e in range(2):
        stack.append(cas(kx, 16 * chip + 2 * line + e - 2, GX) * (line < 10))
    for e in range(2):
        for g in range(4):
            pair = np.where(line < 12, 2 * g + line - 10, 8 + line - 12)
            used = (line >= 10) & (line < (14 if g == 0 else 12))
            stack.append(cas(kx, 16 * chip + 2 * pair + e - 2, GX) * used)
    hx = np.stack(stack).astype(np.float32)
    lane = np.arange(LANES)
    yb, group, yl = lane // 32, lane // 8 % 4, lane % 4
    ky = np.arange(GY)
    parts = [cas(32 * yb + 16 * zh + 4 * group + yl - 2, ky, GY) for zh in range(2)]
    parts += [cas(32 * yb + 16 * zh + 16 + yl - 2, ky, GY) for zh in range(2)]
    hy = np.concatenate(parts, axis=0).astype(np.float32)
    fx, bx = wave_tables(GX)
    fy, by = wave_tables(GY)
    fz, bz = wave_tables(KZ)
    scale = 1.0 / (GX * GY * KZ * math.pi)
    fx_rows = np.broadcast_to(np.stack([fx, bx * scale])[:, :, None], (2, GX, LANES)).astype(np.float32)
    fy_rows = np.stack([fy, by])[:, None, :].astype(np.float32)
    wave = 8 * np.arange(PLANE)[:, None] + (lane // 16)[None, :]
    fz_rows = np.stack([fz[wave], bz[wave]]).astype(np.float32)
    return hz, hx, hx.transpose(0, 2, 1).copy(), hy, hy.T.copy(), cells, fx_rows, fy_rows, fz_rows


def mm(a, b, dims=((1,), (0,))):
    return lax.dot_general(
        a, b, (dims, ((), ())), precision=lax.Precision.HIGHEST, preferred_element_type=jnp.float32
    )


def swap_blocks(tiles):
    tiles = list(tiles)
    count = len(tiles)
    unit = LANES // count
    block = lax.broadcasted_iota(jnp.int32, tiles[0].shape, 1) // unit
    bit = 1
    while bit < count:
        low = block & bit == 0
        for n in range(count):
            if n & bit == 0:
                one, two = tiles[n], tiles[n | bit]
                tiles[n] = jnp.where(low, one, pltpu.roll(two, unit * bit, 1))
                tiles[n | bit] = jnp.where(low, pltpu.roll(one, LANES - unit * bit, 1), two)
        bit *= 2
    return tiles


def spline(fraction):
    previous = {0: jnp.ones_like(fraction)}
    fourth = previous
    for degree in range(2, 6):
        current = {}
        for offset in range(degree):
            abscissa = fraction + float(offset)
            summed = (float(degree) - abscissa) * previous[offset - 1] if offset else None
            if offset in previous:
                term = abscissa * previous[offset]
                summed = term if summed is None else term + summed
            current[offset] = summed * (1.0 / (degree - 1))
        if degree == 4:
            fourth = current
        previous = current
    values = [previous[4 - j] for j in range(5)]
    slopes = []
    for j in range(5):
        low = fourth.get(4 - j)
        high = fourth.get(3 - j)
        slopes.append(-high if low is None else low if high is None else low - high)
    return values, slopes


def kernel(
    field, place, polar, base, lists, hz_hbm, hx_hbm, hx_t_hbm, hy_hbm, hy_t_hbm, cells_hbm, fx, fy, fz,
    out_x, out_r,
    hz, hx, hx_t, hy, hy_t, cells,
    pdx, pdy, pdf, zhat, zhat_t, infl, own, coef, acc, direct, vec, keepv, spectrum,
    dsend0, dsend1, near0, near1, asend, arecv, bsend, brecv, csend, crecv, esend, erecv,
    psend, pplane, psend2, pline,
    send_sem, recv_sem, load_sem,
):
    me_r = lax.axis_index("row")
    me_c = lax.axis_index("col")
    core = lax.rem(me_r, 2)
    me_x = lax.rem(me_c, 4)
    me_y = me_c // 8
    me_h = lax.rem(me_c // 4, 2)
    me_a = me_y * 8 + me_x * 2 + core
    me_z = me_h * 8 + me_r // 2

    def to(dr, dc):
        return (lax.rem(me_r + ROW_STEP[dr], ROWS), lax.rem(me_c + COL_STEP[dc], COLS))

    def plane_device(a):
        return (me_r // 2 * 2 + lax.rem(a, 2), a // 8 * 8 + me_h * 4 + lax.rem(a // 2, 4))

    def line_device(z):
        return (lax.rem(z, 8) * 2 + core, me_y * 8 + z // 8 * 4 + me_x)

    def each_plane(body):
        @pl.loop(1, PLANE)
        def _(k):
            a = lax.rem(me_a + k, PLANE)
            body(a, plane_device(a))

    def each_line(body):
        @pl.loop(1, LINE)
        def _(k):
            off = LINE // 2 + k // 2 * (1 - 2 * lax.rem(k, 2))
            z = lax.rem(me_z + off, LINE)
            body(z, line_device(z))

    barrier = pltpu.get_barrier_semaphore()

    def greet(_, device):
        pl.semaphore_signal(barrier, 1, device_id=device, device_id_type=MESH)

    each_line(greet)
    each_plane(greet)
    for dr, dc in NEIGHBOURS:
        greet(None, to(dr, dc))

    loads = []
    for n, (src, dst) in enumerate(
        ((cells_hbm, cells), (hz_hbm, hz), (hx_hbm, hx), (hy_hbm, hy), (hy_t_hbm, hy_t), (hx_t_hbm, hx_t))
    ):
        loads.append(pltpu.make_async_copy(src, dst, load_sem.at[n]))
        loads[n].start()

    def remote(src, dst, phase, device):
        pltpu.make_async_remote_copy(
            src_ref=src, dst_ref=dst, send_sem=send_sem.at[phase], recv_sem=recv_sem.at[phase],
            device_id=device, device_id_type=MESH,
        ).start()

    def keep(src, dst, phase):
        pltpu.make_async_copy(src, dst, recv_sem.at[phase]).start()

    def arrived(ref, phase):
        pltpu.make_async_copy(ref, ref, recv_sem.at[phase]).wait()

    def left(ref, phase):
        pltpu.make_async_copy(ref, ref, send_sem.at[phase]).wait()

    row_id = lax.broadcasted_iota(jnp.int32, (8, ATOMS), 0)
    alpha = polar[0, 0]
    vec[...] = jnp.zeros((8, ATOMS), jnp.float32)
    for d in range(3):
        vec[2 * d : 2 * d + 2, :] = field[0, 0, d]
    r0 = vec[...]
    d1 = alpha * r0

    atom = lax.broadcasted_iota(jnp.int32, (1, ATOMS), 1)
    origin = ((me_r * CX).astype(jnp.float32), (me_c * CY).astype(jnp.float32), (atom // TILE * (KZ // TILES)).astype(jnp.float32))
    inner_place = [place[0, c] - origin[c] for c in range(3)]
    damper = jnp.exp(jnp.log(alpha) * -0.5)
    for t in range(TILES):
        cut = slice(t * TILE, (t + 1) * TILE)
        for c in range(3):
            dsend0[c, t : t + 1, :] = inner_place[c][:, cut]
        dsend0[3, t : t + 1, :] = damper[:, cut]
        for c in range(6):
            dsend0[4 + c, t : t + 1, :] = d1[c : c + 1, cut]

    vec[...] = jnp.zeros((8, ATOMS), jnp.float32)
    for c in range(3):
        cell = (base[0, c] + 2) & ((GX, GY, KZ)[c] - 1)
        vec[c : c + 1, :] = place[0, c] - cell.astype(jnp.float32)
    values, slopes = spline(vec[...])
    rel_x = ((base[0, 0] - me_r * CX + 2) & (GX - 1)) - 2
    rel_y = ((base[0, 1] - me_c * CY + 2) & (GY - 1)) - 2
    rel_z = base[0, 2]

    def placed(step, row):
        value = jnp.zeros(step.shape, jnp.float32)
        slope = jnp.zeros(step.shape, jnp.float32)
        for j in range(5):
            here = step == j
            value = jnp.where(here, values[j][row : row + 1], value)
            slope = jnp.where(here, slopes[j][row : row + 1], slope)
        return value, slope

    loads[0].wait()
    for g in range(ALL // 32):
        cut = slice(32 * g, 32 * g + 32)
        cell_x = jnp.concatenate([cells[0, cut, :]] * TILES, axis=1)
        cell_y = jnp.concatenate([cells[1, cut, :]] * TILES, axis=1)
        tx, sx = placed(cell_x - rel_x, 0)
        ty, sy = placed(cell_y - rel_y, 1)
        pdx[cut, :] = sx * ty
        pdy[cut, :] = tx * sy
        pdf[cut, :] = tx * ty
    step_z = (lax.broadcasted_iota(jnp.int32, (KZ, ATOMS), 0) - rel_z) & (KZ - 1)
    tz, sz = placed(step_z, 2)
    loads[1].wait()
    zhat[:, 0:ATOMS] = mm(hz[...], tz)
    zhat[:, ATOMS:] = mm(hz[...], sz)
    zhat_t[...] = zhat[...].T

    lane_row = lax.broadcasted_iota(jnp.int32, (1, LANES), 1)
    mine = lane_row == 16 * (me_z // 2)
    row_z = fz[:, pl.ds(me_a, 1), :]
    f_z = jnp.sum(jnp.where(mine, row_z[0], 0.0), axis=1, keepdims=True)
    b_z = jnp.sum(jnp.where(mine, row_z[1], 0.0), axis=1, keepdims=True)
    m2 = fx[0] + (fy[0] + f_z)
    zero = m2 == 0.0
    safe = jnp.where(zero, 1.0, m2)
    shape = jnp.exp(-(math.pi**2 / BETA**2) * safe) / safe * (fx[1] * (fy[1] * b_z))
    infl[...] = jnp.where(zero, 0.0, shape)

    for t in range(TILES):
        cut = slice(t * TILE, (t + 1) * TILE)
        for c in range(4):
            source = THOLE * damper[:, cut] if c == 3 else inner_place[c][:, cut]
            own[t, c] = jnp.broadcast_to(source, (TILE, TILE)).T

    for op in range(2):
        asend[op] = jnp.zeros((PLANE * 16, LANES), jnp.float32)

    def send_near(src, dst, phase):
        for dr, dc in NEIGHBOURS:
            remote(src, dst.at[(1 - dr) * 3 + (1 - dc)], phase, to(dr, dc))
        keep(src, dst.at[4], phase)

    def listed(t, k):
        entry = lists[0, 0, t, k]
        return entry // TILES, lax.rem(entry, TILES)

    def coefficients():
        line = lax.broadcasted_iota(jnp.int32, (TILE, TILE), 0)
        lane = lax.broadcasted_iota(jnp.int32, (TILE, TILE), 1)

        @pl.loop(0, TILES * NBR)
        def _(at):
            t = at // NBR
            k = at - t * NBR
            brick, tile = listed(t, k)
            dr = brick // 3
            shift = (
                (dr - 1) * CX, (brick - 3 * dr - 1) * CY, (lax.rem(tile - t + TILES + 1, TILES) - 1) * (KZ // TILES)
            )
            dx, dy, dz = (
                (near0[brick, c, pl.ds(tile, 1), :] + shift[c].astype(jnp.float32)) - own[t, c] for c in range(3)
            )
            strength = own[t, 3] * near0[brick, 3, pl.ds(tile, 1), :]
            sq = dx * dx + dy * dy + dz * dz
            inv = jnp.where(line + k * TILE == lane, 0.0, lax.rsqrt(sq))
            rho = sq * inv
            damp = jnp.exp(-strength * (sq * rho))
            gauss = jnp.exp(-(BETA * BETA) * sq)
            den = 1.0 + (0.4 * BETA) * rho
            frac = pltpu.reciprocal(den, approx=True)
            frac = frac * (2.0 - den * frac)
            poly = ERFCX[-1] * frac + ERFCX[-2]
            for c in ERFCX[-3::-1]:
                poly = poly * frac + c
            screen = gauss * (frac * poly)
            g = (2.0 * BETA / math.sqrt(math.pi)) * gauss
            i2 = inv * inv
            s1 = ((screen - damp) * inv + g) * i2
            s2 = (3.0 * (s1 - strength * damp) + (2.0 * BETA * BETA) * g) * i2
            ax, ay, az = s2 * dx, s2 * dy, s2 * dz
            coef[at, 0] = ax * dx - s1
            coef[at, 1] = ax * dy
            coef[at, 2] = ax * dz
            coef[at, 3] = ay * dy - s1
            coef[at, 4] = ay * dz
            coef[at, 5] = az * dz - s1

    def pairs(near, first_row):
        block = 32
        blocks = TILE // block

        @pl.loop(0, TILES * blocks)
        def _(unit):
            t = unit // blocks
            cut = pl.ds(pl.multiple_of((unit - t * blocks) * block, block), block)

            def step(k, sums):
                brick, tile = listed(t, k)
                xx, xy, xz, yy, yz, zz = (coef[t * NBR + k, c, cut, :] for c in range(6))
                out = []
                for s in range(2):
                    vx, vy, vz = (near[brick, first_row + 2 * c + s, pl.ds(tile, 1), :] for c in range(3))
                    out.append(sums[3 * s] + (xx * vx + xy * vy + xz * vz))
                    out.append(sums[3 * s + 1] + (xy * vx + yy * vy + yz * vz))
                    out.append(sums[3 * s + 2] + (xz * vx + yz * vy + zz * vz))
                return tuple(out)

            zero = jnp.zeros((block, TILE), jnp.float32)
            sums = lax.fori_loop(0, NBR, step, (zero,) * 6, unroll=6)
            for c in range(6):
                acc[t, c, cut, :] = sums[c]

    def finish_pairs():
        direct[...] = jnp.zeros((8, ATOMS), jnp.float32)
        for t in range(TILES):
            for s in range(2):
                for d in range(3):
                    total = jnp.sum(acc[t, 3 * s + d].T, axis=0, keepdims=True)
                    direct[2 * d + s : 2 * d + s + 1, t * TILE : (t + 1) * TILE] = total

    def by_rhs(v, d):
        choice = [jnp.broadcast_to(v[2 * d + s : 2 * d + s + 1], (8, ATOMS)) for s in range(2)]
        return jnp.concatenate(choice * SLOTS, axis=0)

    def fold_rows(product, s):
        total = None
        for slot in range(SLOTS):
            piece = product[16 * slot + 8 * s : 16 * slot + 8 * s + 8]
            total = piece if total is None else total + piece
        return jnp.sum(total, axis=0, keepdims=True)

    def inner(left_v, right_v, s):
        product = jnp.where(row_id & 1 == s, left_v * right_v, 0.0)
        return jnp.sum(jnp.sum(product, axis=0, keepdims=True), axis=1, keepdims=True)

    def pack(numbers):
        out = jnp.zeros((1, LANES), jnp.float32)
        for n, value in enumerate(numbers):
            out = jnp.where(lane_row == n, value, out)
        return out

    def unpack(line, n):
        return jnp.sum(jnp.where(lane_row == n, line, 0.0), axis=1, keepdims=True)

    def sum_planes(op, line):
        psend[op] = line
        phase = 10 + 2 * op
        each_plane(lambda a, device: remote(psend.at[op], pplane.at[op, me_a], phase, device))
        keep(psend.at[op], pplane.at[op, me_a], phase)

    def sum_lines(op):
        arrived(pplane.at[op], 10 + 2 * op)
        psend2[op] = jnp.sum(pplane[op], axis=0)
        phase = 11 + 2 * op
        each_line(lambda z, device: remote(psend2.at[op], pline.at[op, me_z], phase, device))
        keep(psend2.at[op], pline.at[op, me_z], phase)

    def sum_done(op):
        arrived(pline.at[op], 11 + 2 * op)
        return jnp.sum(pline[op], axis=0)

    lane_wide = lax.broadcasted_iota(jnp.int32, (GX, 2 * LANES), 1)
    x_bit = lane_wide // 4 & 1 == 0
    group = lane_wide // 8 & 3

    def spread(op, v):
        phase = 5 * op
        flat = by_rhs(v, 0) * pdx[...] + by_rhs(v, 1) * pdy[...]
        steep = by_rhs(v, 2) * pdf[...]
        charge = mm(flat, zhat_t[0:ATOMS, :]) + mm(steep, zhat_t[ATOMS:, :])
        waves = jnp.concatenate([charge, jnp.zeros((KZ - ALL, KZ), jnp.float32)], axis=0).T
        tiles = []
        for i in range(8):
            piece = waves[PLANE * i : PLANE * i + PLANE]
            tiles.append(jnp.concatenate([piece[:, 0:LANES], piece[:, LANES:]], axis=0))
        tiles = swap_blocks(tiles)
        for slot in range(SLOTS):
            part = tiles[slot % 8][slot // 8 * PLANE : slot // 8 * PLANE + PLANE]
            asend[op, pl.ds(SLOT_ROW[slot], PLANE, stride=16), :] = part

    def send_planes(op):
        phase = 5 * op
        mine = arecv.at[op, pl.ds(me_a * 16, 16)]
        each_plane(lambda a, device: remote(asend.at[op, pl.ds(a * 16, 16)], mine, phase + 1, device))
        keep(asend.at[op, pl.ds(me_a * 16, 16)], mine, phase + 1)

    row8 = lax.broadcasted_iota(jnp.int32, (8, LANES), 0)

    def gather_planes(op):
        phase = 5 * op
        arrived(arecv.at[op], phase + 1)

        def got(yb, x, one_core, yh):
            at = (yb * 8 + x * 2 + one_core) * 16 + yh * 8
            return arecv[op, at : at + 8, :]

        def joined(low, high):
            high = pltpu.roll(high, 4, 0)
            return jnp.where(row8 < 4, low, jnp.where(row8 < 6, low + high, high)), high

        tiles = []
        for yb in range(4):
            last0, last1 = joined(got(yb, 3, 0, 1), got(yb, 3, 1, 1))
            for g in range(4):
                low, high = got(yb, g, 0, 0), got(yb, g, 1, 0)
                if g:
                    low, high = low + got(yb, g - 1, 0, 1), high + got(yb, g - 1, 1, 1)
                tile0, tile1 = joined(low, high)
                edge = last0 if g == 1 else pltpu.roll(last0, (2 - 2 * g) % 8, 0)
                rest = pltpu.roll(last1, 4, 0) if g == 0 else 0.0
                tile1 = jnp.where(
                    row8 < 2, tile1, jnp.where(row8 < 4, edge, jnp.where(row8 < 6, rest, 0.0))
                )
                tiles.append(jnp.concatenate([tile0, tile1], axis=0))
        tiles = swap_blocks(tiles)
        for n in range(LINE):
            bsend[op, n] = tiles[n]
        each_line(lambda z, device: remote(bsend.at[op, z], brecv.at[op, me_z], phase + 2, device))
        keep(bsend.at[op, me_z], brecv.at[op, me_z], phase + 2)

    def convolve(op):
        phase = 5 * op
        arrived(brecv.at[op], phase + 2)
        lines = jnp.concatenate(
            [brecv[op, 0:8].reshape(GX, LANES), brecv[op, 8:16].reshape(GX, LANES)], axis=1
        )
        part = [mm(hx[n], lines) for n in range(10)]
        body = jnp.where(x_bit, part[0], part[1])
        edge = jnp.where(x_bit, part[2], part[6])
        for g in range(1, 4):
            edge = jnp.where(group == g, jnp.where(x_bit, part[2 + g], part[6 + g]), edge)
        waves = mm(jnp.concatenate([body, edge], axis=1), hy[...])
        spectrum[op] = waves
        back = mm(infl[...] * waves, hy_t[...])
        body, edge = back[:, 0 : 2 * LANES], back[:, 2 * LANES :]
        out = jnp.where(x_bit, mm(hx_t[0], body), mm(hx_t[1], body))
        for g in range(4):
            piece = jnp.where(x_bit, mm(hx_t[2 + g], edge), mm(hx_t[6 + g], edge))
            out = out + jnp.where(group == g, piece, 0.0)
        csend[op, 0:8] = out[:, 0:LANES].reshape(8, 16, LANES)
        csend[op, 8:16] = out[:, LANES:].reshape(8, 16, LANES)
        each_line(lambda z, device: remote(csend.at[op, z], crecv.at[op, me_z], phase + 3, device))
        keep(csend.at[op, me_z], crecv.at[op, me_z], phase + 3)

    def scatter_planes(op):
        phase = 5 * op
        arrived(crecv.at[op], phase + 3)
        tiles = swap_blocks([crecv[op, n] for n in range(LINE)])
        for yb in range(4):
            ends = [(tiles[4 * yb + g][0:8], tiles[4 * yb + g][8:16]) for g in range(4)]
            edges = [
                ends[g][1] if g == 1 else pltpu.roll(ends[g][1], (2 * g - 2) % 8, 0) for g in range(4)
            ]
            last0 = jnp.where(
                row8 < 2, edges[0], jnp.where(row8 < 4, edges[1], jnp.where(row8 < 6, edges[2], edges[3]))
            )
            ends.append((last0, pltpu.roll(ends[0][1], 4, 0)))
            for n, (one, two) in enumerate(ends):
                high = jnp.where(row8 < 4, pltpu.roll(one, 4, 0), pltpu.roll(two, 4, 0))
                for x, yh in ((n, 0), (n - 1, 1)):
                    if 0 <= x < 4:
                        at = (yb * 8 + x * 2) * 16 + yh * 8
                        esend[op, at : at + 8, :] = one
                        esend[op, at + 16 : at + 24, :] = high
        mine = erecv.at[op, pl.ds(me_a * 16, 16)]
        each_plane(lambda a, device: remote(esend.at[op, pl.ds(a * 16, 16)], mine, phase + 4, device))
        keep(esend.at[op, pl.ds(me_a * 16, 16)], mine, phase + 4)

    def sample(op):
        phase = 5 * op
        arrived(erecv.at[op], phase + 4)
        none = jnp.zeros((PLANE, LANES), jnp.float32)
        tiles = []
        for slot in range(8):
            one = erecv[op, pl.ds(SLOT_ROW[slot], PLANE, stride=16), :]
            two = erecv[op, pl.ds(SLOT_ROW[slot + 8], PLANE, stride=16), :] if slot < 4 else none
            tiles.append(jnp.concatenate([one, two], axis=0))
        tiles = swap_blocks(tiles)
        waves = jnp.concatenate(
            [jnp.concatenate([tile[0:PLANE], tile[PLANE:]], axis=1) for tile in tiles], axis=0
        )
        whole = waves.T[0:ALL]
        level = mm(whole, zhat[:, 0:ATOMS])
        steep = mm(whole, zhat[:, ATOMS:])
        parts = (level * pdx[...], level * pdy[...], steep * pdf[...])
        vec[...] = jnp.zeros((8, ATOMS), jnp.float32)
        for s in range(2):
            for d in range(3):
                vec[2 * d + s : 2 * d + s + 1, :] = fold_rows(parts[d], s)
        return vec[...]

    def wide(numbers):
        row = lax.broadcasted_iota(jnp.int32, (8, 1), 0)
        return jnp.where(row & 1 == 0, numbers[0], numbers[1])

    def near_part(v):
        return v / alpha - SELF * v

    spread(0, d1)
    pl.semaphore_wait(barrier, PLANE - 1 + LINE - 1 + 8)
    send_planes(0)
    send_near(dsend0, near0, 0)
    gather_planes(0)
    arrived(near0, 0)
    coefficients()
    for load in loads[2:]:
        load.wait()
    convolve(0)
    pairs(near0, 4)
    finish_pairs()
    scatter_planes(0)
    recip = sample(0)
    direct1 = direct[...]
    q1 = near_part(d1) - direct1 + recip
    w1 = alpha * q1
    keepv[0] = direct1
    keepv[1] = q1
    keepv[2] = w1

    spread(1, w1)
    send_planes(1)
    for c in range(6):
        for t in range(TILES):
            dsend1[c, t : t + 1, :] = w1[c : c + 1, t * TILE : (t + 1) * TILE]
    send_near(dsend1, near1, 5)
    products = [inner(u, v, s) for u, v in ((r0, d1), (d1, q1), (q1, w1)) for s in range(2)]
    sum_planes(0, pack(products))
    gather_planes(1)
    sum_lines(0)
    arrived(near1, 5)
    pairs(near1, 0)
    finish_pairs()
    convolve(1)
    line = sum_done(0)
    progress = [unpack(line, s) for s in range(2)]
    step = [progress[s] / unpack(line, 2 + s) for s in range(2)]
    following = [step[s] * step[s] * unpack(line, 4 + s) - progress[s] for s in range(2)]
    ratio = [following[s] / progress[s] for s in range(2)]
    step_w = wide(step)
    grown = 1.0 + wide(ratio)
    direct2 = grown * keepv[0] - step_w * direct[...]
    d2 = grown * d1 - step_w * keepv[2]
    local_part = near_part(d2) - direct2
    here = lax.rem(me_z, 2) == 0
    waves = jnp.where(here, 1.0 + ratio[0], 1.0 + ratio[1]) * spectrum[0]
    waves = waves - jnp.where(here, step[0], step[1]) * spectrum[1]
    power = jnp.sum(jnp.sum(infl[...] * (waves * waves), axis=0, keepdims=True), axis=1, keepdims=True)
    products = [inner(d2, local_part, s) for s in range(2)]
    sum_planes(1, pack(products) + jnp.where(lane_row == lax.rem(me_z, 2), power, 0.0))
    sum_lines(1)
    scatter_planes(1)
    w1 = keepv[2]
    z1 = near_part(w1) - direct[...] + sample(1)
    q1 = keepv[1]
    d2 = grown * d1 - step_w * w1
    q2 = grown * q1 - step_w * z1
    x1 = step_w * d1
    r1 = r0 - step_w * q1
    line = sum_done(1)
    step2 = wide([following[s] / unpack(line, s) for s in range(2)])
    x2 = x1 + step2 * d2
    r2 = r1 - step2 * q2
    for d in range(3):
        out_x[0, 0, d] = x2[2 * d : 2 * d + 2]
        out_r[0, 0, d] = r2[2 * d : 2 * d + 2]

    left(near0.at[pl.ds(0, 8)], 0)
    left(near1.at[pl.ds(0, 8)], 5)
    for op in range(2):
        left(arecv.at[op, pl.ds(0, (PLANE - 1) * 16)], 5 * op + 1)
        left(brecv.at[op, pl.ds(0, LINE - 1)], 5 * op + 2)
        left(crecv.at[op, pl.ds(0, LINE - 1)], 5 * op + 3)
        left(erecv.at[op, pl.ds(0, (PLANE - 1) * 16)], 5 * op + 4)
        left(pplane.at[op, pl.ds(0, PLANE - 1)], 10 + 2 * op)
        left(pline.at[op, pl.ds(0, LINE - 1)], 11 + 2 * op)


def local(field, place, polar, base, lists):
    vmem = pl.BlockSpec(memory_space=pltpu.VMEM)
    smem = pl.BlockSpec(memory_space=pltpu.SMEM)
    f32 = jnp.float32

    def buf(*shape):
        return pltpu.VMEM(shape, f32)

    tables = constants()
    hz, hx, hx_t, hy, hy_t, cells = tables[:6]
    out = jax.ShapeDtypeStruct((1, 1, 3, 2, ATOMS), f32)
    x, r = pl.pallas_call(
        kernel,
        out_shape=(out, out),
        in_specs=[vmem] * 4 + [smem] + [pl.BlockSpec(memory_space=pl.ANY)] * 6 + [vmem] * 3,
        out_specs=(vmem, vmem),
        scratch_shapes=[
            buf(*hz.shape), buf(*hx.shape), buf(*hx_t.shape), buf(*hy.shape), buf(*hy_t.shape),
            pltpu.VMEM(cells.shape, jnp.int32),
            buf(ALL, ATOMS), buf(ALL, ATOMS), buf(ALL, ATOMS),
            buf(KZ, 2 * ATOMS), buf(2 * ATOMS, KZ), buf(GX, LANES),
            buf(TILES, 4, TILE, TILE), buf(TILES * NBR, 6, TILE, TILE), buf(TILES, 6, TILE, TILE),
            buf(8, ATOMS), buf(8, ATOMS), buf(3, 8, ATOMS), buf(2, GX, GY),
            buf(10, TILES, TILE), buf(6, TILES, TILE), buf(9, 10, TILES, TILE), buf(9, 6, TILES, TILE),
            buf(2, PLANE * 16, LANES), buf(2, PLANE * 16, LANES),
            buf(2, LINE, 16, LANES), buf(2, LINE, 16, LANES), buf(2, LINE, 16, LANES), buf(2, LINE, 16, LANES),
            buf(2, PLANE * 16, LANES), buf(2, PLANE * 16, LANES),
            buf(2, 1, LANES), buf(2, PLANE, 1, LANES), buf(2, 1, LANES), buf(2, LINE, 1, LANES),
            pltpu.SemaphoreType.DMA((14,)), pltpu.SemaphoreType.DMA((14,)), pltpu.SemaphoreType.DMA((6,)),
        ],
        compiler_params=pltpu.CompilerParams(
            collective_id=0, has_side_effects=True, vmem_limit_bytes=56 * 1024 * 1024
        ),
    )(
        field.transpose(0, 1, 3, 2, 4), place.transpose(0, 2, 1, 3), polar.reshape(1, 1, 1, ATOMS),
        base.transpose(0, 2, 1, 3), lists, *(jnp.asarray(c) for c in tables),
    )
    return x.transpose(0, 1, 3, 2, 4), r.transpose(0, 1, 3, 2, 4)


def solution(mesh):
    placed = (
        P("row", "col", None, None, None),
        P("row", "col", None, None),
        P("row", "col", None),
        P("row", "col", None, None),
        P("row", "col", None, None),
    )
    return jax.shard_map(
        local,
        mesh=mesh,
        in_specs=placed,
        out_specs=(P("row", "col", None, None, None), P("row", "col", None, None, None)),
        check_vma=False,
    )
```

time: 122 us -> 104 us (0.85)
  Pallas kernels: 117 us -> 101 us
  local copies, waits for them, and re-layouts: 4.45 us -> 1.92 us
    pallas_call x1, Pallas kernels: 117 us -> 101 us  [local(): pl.pallas_call(kernel, out_shape=(out, out), in_specs=[vmem] * 4 + [smem]...]
    pallas_call x2 -> x0, local copies, waits for them, and re-layouts: 1.93 us -> none  [local(): pl.pallas_call(kernel, out_shape=(out, out), in_specs=[vmem] * 4 + [smem]...]
    unnamed x9 -> x4, local copies, waits for them, and re-layouts: 2.52 us -> 1.92 us
where the time goes in v3:
time: 104 us
  Pallas kernels  101 us (97%)
  local copies, waits for them, and re-layouts  1.92 us (2%)
    pallas_call x1, Pallas kernels, local(): pl.pallas_call(kernel, out_shape=(out, out), in_specs=[vmem] * 4 + [smem]...  101 us

profile of v3, /device:TPU:1, one launch (start us, length us, event | category | flops | bytes accessed | tf_op | source)
XLA Modules:
  0.0 103.8 jit_solution(15542275697758027372)
XLA Ops:
  0.6 101.2 %shard_map.149 = (f32[1,1,3,2,512]{4,3,2,1,0:T(2,128)}, f32[1,1,3,2,512]{4,3,2,1,0:T(2,128)}) custom-call(f32[1,1,3,2,512]{4,3,2,1,0:T(2,128)} %bitcast.6, f32[1,3,1,512]{3,2,1,0:T(1,128)} %bitcast.9, f32[1,1,1,512]{3,2,1,0:T(1,128)} %bitcast.11, s32[1,3,1,512]{3,2,1,0:T(1,128)} %bitcast.10, s32[1,1,4,12]{3,2,1,0:T(4,128)} %lists.1, ...), custom_call_target="tpu_custom_call" | custom-call | tf_op jit(solution)/shard_map/pallas_call | solution.py:660
  101.9 0.0 copy-start
  101.9 1.3 %copy.18 = f32[1,1,2,3,512]{4,2,3,1,0:T(2,128)} copy(f32[1,1,2,3,512]{4,2,3,1,0:T(2,128)} %bitcast.8) | data formatting | bytes 24576
  103.2 0.0 copy-done
  103.2 0.6 copy.19
Async XLA Ops:
  101.9 1.3 %copy-start = (f32[1,1,3,2,512]{4,3,2,1,0:T(2,128)S(1)}, f32[1,1,3,2,512]{4,3,2,1,0:T(2,128)}, u32[]{:S(2)}) copy-start(f32[1,1,3,2,512]{4,3,2,1,0:T(2,128)} %get-tuple-element.5) | copy-start | bytes 36868

commit v4 on v3

--- a/solution.py
+++ b/solution.py
@@ -109,13 +109,27 @@
     fy_rows = np.stack([fy, by])[:, None, :].astype(np.float32)
     wave = 8 * np.arange(PLANE)[:, None] + (lane // 16)[None, :]
     fz_rows = np.stack([fz[wave], bz[wave]]).astype(np.float32)
-    return hz, hx, hx.transpose(0, 2, 1).copy(), hy, hy.T.copy(), cells, fx_rows, fy_rows, fz_rows
-
-
-def mm(a, b, dims=((1,), (0,))):
-    return lax.dot_general(
-        a, b, (dims, ((), ())), precision=lax.Precision.HIGHEST, preferred_element_type=jnp.float32
-    )
+
+    def two(x):
+        high = x.astype(jnp.bfloat16)
+        return np.stack([high, (x - high.astype(np.float32)).astype(jnp.bfloat16)])
+
+    hx_t = np.ascontiguousarray(hx.transpose(0, 2, 1))
+    hy_t = np.ascontiguousarray(hy.T)
+    return two(hz), two(hx), two(hx_t), two(hy), two(hy_t), cells, fx_rows, fy_rows, fz_rows
+
+
+def halves(x):
+    high = x.astype(jnp.bfloat16)
+    return high, (x - high.astype(jnp.float32)).astype(jnp.bfloat16)
+
+
+def dot(a, b):
+    return jnp.dot(a, b, preferred_element_type=jnp.float32)
+
+
+def mm(a, b):
+    return (dot(a[1], b[0]) + dot(a[0], b[1])) + dot(a[0], b[0])
 
 
 def swap_blocks(tiles):
@@ -163,7 +177,7 @@
     field, place, polar, base, lists, hz_hbm, hx_hbm, hx_t_hbm, hy_hbm, hy_t_hbm, cells_hbm, fx, fy, fz,
     out_x, out_r,
     hz, hx, hx_t, hy, hy_t, cells,
-    pdx, pdy, pdf, zhat, zhat_t, infl, own, coef, acc, direct, vec, keepv, spectrum,
+    pdx, pdy, pdf, zhat, zhat_t, pick, infl, own, coef, acc, direct, vec, keepv, spectrum,
     dsend0, dsend1, near0, near1, asend, arecv, bsend, brecv, csend, crecv, esend, erecv,
     psend, pplane, psend2, pline,
     send_sem, recv_sem, load_sem,
@@ -186,18 +200,27 @@
     def line_device(z):
         return (lax.rem(z, 8) * 2 + core, me_y * 8 + z // 8 * 4 + me_x)
 
+    plane_targets = []
+    for far in range(4, -1, -1):
+        for ky in range(4):
+            for kx in range(4):
+                if min(ky, 4 - ky) + min(kx, 4 - kx) == far:
+                    for kc in range(2):
+                        if ky or kx or kc:
+                            a = lax.rem(me_y + ky, 4) * 8 + lax.rem(me_x + kx, 4) * 2 + lax.rem(core + kc, 2)
+                            plane_targets.append((a, plane_device(a)))
+    line_targets = []
+    for k in range(1, LINE):
+        z = lax.rem(me_z + LINE // 2 + k // 2 * (1 - 2 * (k % 2)), LINE)
+        line_targets.append((z, line_device(z)))
+
     def each_plane(body):
-        @pl.loop(1, PLANE)
-        def _(k):
-            a = lax.rem(me_a + k, PLANE)
-            body(a, plane_device(a))
+        for a, device in plane_targets:
+            body(a, device)
 
     def each_line(body):
-        @pl.loop(1, LINE)
-        def _(k):
-            off = LINE // 2 + k // 2 * (1 - 2 * lax.rem(k, 2))
-            z = lax.rem(me_z + off, LINE)
-            body(z, line_device(z))
+        for z, device in line_targets:
+            body(z, device)
 
     barrier = pltpu.get_barrier_semaphore()
 
@@ -282,9 +305,17 @@
     step_z = (lax.broadcasted_iota(jnp.int32, (KZ, ATOMS), 0) - rel_z) & (KZ - 1)
     tz, sz = placed(step_z, 2)
     loads[1].wait()
-    zhat[:, 0:ATOMS] = mm(hz[...], tz)
-    zhat[:, ATOMS:] = mm(hz[...], sz)
-    zhat_t[...] = zhat[...].T
+    waves = (hz[0], hz[1])
+    for n, table in enumerate((tz, sz)):
+        cut = slice(n * ATOMS, (n + 1) * ATOMS)
+        result = mm(waves, halves(table))
+        zhat[0, :, cut], zhat[1, :, cut] = halves(result)
+        zhat_t[0, cut, :], zhat_t[1, cut, :] = halves(result.T)
+    block_row = lax.broadcasted_iota(jnp.int32, (TILE, LANES), 1)
+    for t in range(TILES):
+        for r in range(6):
+            at = (6 * t + r) * TILE
+            pick[at : at + TILE, :] = jnp.where(block_row == 8 * t + r, 1.0, 0.0).astype(jnp.bfloat16)
 
     lane_row = lax.broadcasted_iota(jnp.int32, (1, LANES), 1)
     mine = lane_row == 16 * (me_z // 2)
@@ -378,16 +409,16 @@
 
             zero = jnp.zeros((block, TILE), jnp.float32)
             sums = lax.fori_loop(0, NBR, step, (zero,) * 6, unroll=6)
-            for c in range(6):
-                acc[t, c, cut, :] = sums[c]
-
-    def finish_pairs():
-        direct[...] = jnp.zeros((8, ATOMS), jnp.float32)
-        for t in range(TILES):
             for s in range(2):
                 for d in range(3):
-                    total = jnp.sum(acc[t, 3 * s + d].T, axis=0, keepdims=True)
-                    direct[2 * d + s : 2 * d + s + 1, t * TILE : (t + 1) * TILE] = total
+                    acc[t, 2 * d + s, cut, :] = sums[3 * s + d]
+
+    def finish_pairs():
+        wide_sums = jnp.concatenate([acc[t, r] for t in range(TILES) for r in range(6)], axis=1)
+        high, low = halves(wide_sums)
+        totals = (dot(low, pick[...]) + dot(high, pick[...])).T
+        for t in range(TILES):
+            direct[:, t * TILE : (t + 1) * TILE] = totals[8 * t : 8 * t + 8]
 
     def by_rhs(v, d):
         choice = [jnp.broadcast_to(v[2 * d + s : 2 * d + s + 1], (8, ATOMS)) for s in range(2)]
@@ -438,7 +469,7 @@
         phase = 5 * op
         flat = by_rhs(v, 0) * pdx[...] + by_rhs(v, 1) * pdy[...]
         steep = by_rhs(v, 2) * pdf[...]
-        charge = mm(flat, zhat_t[0:ATOMS, :]) + mm(steep, zhat_t[ATOMS:, :])
+        charge = mm(halves(jnp.concatenate([flat, steep], axis=1)), (zhat_t[0], zhat_t[1]))
         waves = jnp.concatenate([charge, jnp.zeros((KZ - ALL, KZ), jnp.float32)], axis=0).T
         tiles = []
         for i in range(8):
@@ -495,18 +526,23 @@
         lines = jnp.concatenate(
             [brecv[op, 0:8].reshape(GX, LANES), brecv[op, 8:16].reshape(GX, LANES)], axis=1
         )
-        part = [mm(hx[n], lines) for n in range(10)]
+        lines = halves(lines)
+        part = [mm((hx[0, n], hx[1, n]), lines) for n in range(10)]
         body = jnp.where(x_bit, part[0], part[1])
         edge = jnp.where(x_bit, part[2], part[6])
         for g in range(1, 4):
             edge = jnp.where(group == g, jnp.where(x_bit, part[2 + g], part[6 + g]), edge)
-        waves = mm(jnp.concatenate([body, edge], axis=1), hy[...])
+        waves = mm(halves(jnp.concatenate([body, edge], axis=1)), (hy[0], hy[1]))
         spectrum[op] = waves
-        back = mm(infl[...] * waves, hy_t[...])
-        body, edge = back[:, 0 : 2 * LANES], back[:, 2 * LANES :]
-        out = jnp.where(x_bit, mm(hx_t[0], body), mm(hx_t[1], body))
+        back = mm(halves(infl[...] * waves), (hy_t[0], hy_t[1]))
+        body, edge = halves(back[:, 0 : 2 * LANES]), halves(back[:, 2 * LANES :])
+
+        def back_x(n, lines):
+            return mm((hx_t[0, n], hx_t[1, n]), lines)
+
+        out = jnp.where(x_bit, back_x(0, body), back_x(1, body))
         for g in range(4):
-            piece = jnp.where(x_bit, mm(hx_t[2 + g], edge), mm(hx_t[6 + g], edge))
+            piece = jnp.where(x_bit, back_x(2 + g, edge), back_x(6 + g, edge))
             out = out + jnp.where(group == g, piece, 0.0)
         csend[op, 0:8] = out[:, 0:LANES].reshape(8, 16, LANES)
         csend[op, 8:16] = out[:, LANES:].reshape(8, 16, LANES)
@@ -550,9 +586,8 @@
         waves = jnp.concatenate(
             [jnp.concatenate([tile[0:PLANE], tile[PLANE:]], axis=1) for tile in tiles], axis=0
         )
-        whole = waves.T[0:ALL]
-        level = mm(whole, zhat[:, 0:ATOMS])
-        steep = mm(whole, zhat[:, ATOMS:])
+        whole = mm(halves(waves.T[0:ALL]), (zhat[0], zhat[1]))
+        level, steep = whole[:, 0:ATOMS], whole[:, ATOMS:]
         parts = (level * pdx[...], level * pdy[...], steep * pdf[...])
         vec[...] = jnp.zeros((8, ATOMS), jnp.float32)
         for s in range(2):
@@ -654,6 +689,9 @@
     def buf(*shape):
         return pltpu.VMEM(shape, f32)
 
+    def half(*shape):
+        return pltpu.VMEM(shape, jnp.bfloat16)
+
     tables = constants()
     hz, hx, hx_t, hy, hy_t, cells = tables[:6]
     out = jax.ShapeDtypeStruct((1, 1, 3, 2, ATOMS), f32)
@@ -663,10 +701,10 @@
         in_specs=[vmem] * 4 + [smem] + [pl.BlockSpec(memory_space=pl.ANY)] * 6 + [vmem] * 3,
         out_specs=(vmem, vmem),
         scratch_shapes=[
-            buf(*hz.shape), buf(*hx.shape), buf(*hx_t.shape), buf(*hy.shape), buf(*hy_t.shape),
+            half(*hz.shape), half(*hx.shape), half(*hx_t.shape), half(*hy.shape), half(*hy_t.shape),
             pltpu.VMEM(cells.shape, jnp.int32),
             buf(ALL, ATOMS), buf(ALL, ATOMS), buf(ALL, ATOMS),
-            buf(KZ, 2 * ATOMS), buf(2 * ATOMS, KZ), buf(GX, LANES),
+            half(2, KZ, 2 * ATOMS), half(2, 2 * ATOMS, KZ), half(TILES * 6 * TILE, LANES), buf(GX, LANES),
             buf(TILES, 4, TILE, TILE), buf(TILES * NBR, 6, TILE, TILE), buf(TILES, 6, TILE, TILE),
             buf(8, ATOMS), buf(8, ATOMS), buf(3, 8, ATOMS), buf(2, GX, GY),
             buf(10, TILES, TILE), buf(6, TILES, TILE), buf(9, 10, TILES, TILE), buf(9, 6, TILES, TILE),

time: 104 us -> 98.6 us (0.948)
  Pallas kernels: 101 us -> 95.8 us
    pallas_call x1, Pallas kernels: 101 us -> 95.8 us  [local(): pl.pallas_call(kernel, out_shape=(out, out), in_specs=[vmem] * 4 + [smem]...]
where the time goes in v4:
time: 98.6 us; the launch traced here: 98.4 us
  Pallas kernels  95.8 us (97%)
  local copies, waits for them, and re-layouts  1.92 us (2%)
    pallas_call x1, Pallas kernels, local(): pl.pallas_call(kernel, out_shape=(out, out), in_specs=[vmem] * 4 + [smem]...  95.8 us

profile of v4, /device:TPU:1, one launch (start us, length us, event | category | flops | bytes accessed | tf_op | source)
XLA Modules:
  0.0 98.4 jit_solution(7914826830414265415)
XLA Ops:
  0.6 95.8 %shard_map.149 = (f32[1,1,3,2,512]{4,3,2,1,0:T(2,128)}, f32[1,1,3,2,512]{4,3,2,1,0:T(2,128)}) custom-call(f32[1,1,3,2,512]{4,3,2,1,0:T(2,128)} %bitcast.6, f32[1,3,1,512]{3,2,1,0:T(1,128)} %bitcast.9, f32[1,1,1,512]{3,2,1,0:T(1,128)} %bitcast.11, s32[1,3,1,512]{3,2,1,0:T(1,128)} %bitcast.10, s32[1,1,4,12]{3,2,1,0:T(4,128)} %lists.1, ...), custom_call_target="tpu_custom_call" | custom-call | tf_op jit(solution)/shard_map/pallas_call | solution.py:698
  96.5 0.0 copy-start
  96.5 1.3 %copy.18 = f32[1,1,2,3,512]{4,2,3,1,0:T(2,128)} copy(f32[1,1,2,3,512]{4,2,3,1,0:T(2,128)} %bitcast.8) | data formatting | bytes 24576
  97.8 0.0 copy-done
  97.8 0.6 copy.19
Async XLA Ops:
  96.5 1.3 %copy-start = (f32[1,1,3,2,512]{4,3,2,1,0:T(2,128)S(1)}, f32[1,1,3,2,512]{4,3,2,1,0:T(2,128)}, u32[]{:S(2)}) copy-start(f32[1,1,3,2,512]{4,3,2,1,0:T(2,128)} %get-tuple-element.5) | copy-start | bytes 36868

commit v5 on v4

--- a/solution.py
+++ b/solution.py
@@ -58,7 +58,10 @@
 
 REGION = region_rows()
 ALL = len(REGION)
-SLOT_ROW = [slot // 6 * 8 + slot % 6 for slot in range(SLOTS)]
+BRICK_ROWS = SLOTS
+LINE_ROWS = 13
+PAIR_UNITS = 16
+PAIRS_AHEAD = (4, 11)
 
 
 def cas(rows, cols, length):
@@ -91,8 +94,8 @@
         stack.append(cas(kx, 16 * chip + 2 * line + e - 2, GX) * (line < 10))
     for e in range(2):
         for g in range(4):
-            pair = np.where(line < 12, 2 * g + line - 10, 8 + line - 12)
-            used = (line >= 10) & (line < (14 if g == 0 else 12))
+            pair = np.where(line < 12, 2 * g + line - 10, 8 + g)
+            used = (line >= 10) & (line < (13 if g < 2 else 12))
             stack.append(cas(kx, 16 * chip + 2 * pair + e - 2, GX) * used)
     hx = np.stack(stack).astype(np.float32)
     lane = np.arange(LANES)
@@ -178,7 +181,7 @@
     out_x, out_r,
     hz, hx, hx_t, hy, hy_t, cells,
     pdx, pdy, pdf, zhat, zhat_t, pick, infl, own, coef, acc, direct, vec, keepv, spectrum,
-    dsend0, dsend1, near0, near1, asend, arecv, bsend, brecv, csend, crecv, esend, erecv,
+    dstat, dsend0, dsend1, nears, near0, near1, asend, arecv, bsend, brecv, csend, crecv, esend, erecv,
     psend, pplane, psend2, pline,
     send_sem, recv_sem, load_sem,
 ):
@@ -227,10 +230,13 @@
     def greet(_, device):
         pl.semaphore_signal(barrier, 1, device_id=device, device_id_type=MESH)
 
+    for op in range(2):
+        for z in range(LINE):
+            brecv[op, 16 * z + 8 : 16 * z + 16, :] = jnp.zeros((8, LANES), jnp.float32)
+    for dr, dc in NEIGHBOURS:
+        greet(None, to(dr, dc))
     each_line(greet)
     each_plane(greet)
-    for dr, dc in NEIGHBOURS:
-        greet(None, to(dr, dc))
 
     loads = []
     for n, (src, dst) in enumerate(
@@ -269,10 +275,10 @@
     for t in range(TILES):
         cut = slice(t * TILE, (t + 1) * TILE)
         for c in range(3):
-            dsend0[c, t : t + 1, :] = inner_place[c][:, cut]
-        dsend0[3, t : t + 1, :] = damper[:, cut]
+            dstat[c, t : t + 1, :] = inner_place[c][:, cut]
+        dstat[3, t : t + 1, :] = damper[:, cut]
         for c in range(6):
-            dsend0[4 + c, t : t + 1, :] = d1[c : c + 1, cut]
+            dsend0[c, t : t + 1, :] = d1[c : c + 1, cut]
 
     vec[...] = jnp.zeros((8, ATOMS), jnp.float32)
     for c in range(3):
@@ -334,9 +340,6 @@
             source = THOLE * damper[:, cut] if c == 3 else inner_place[c][:, cut]
             own[t, c] = jnp.broadcast_to(source, (TILE, TILE)).T
 
-    for op in range(2):
-        asend[op] = jnp.zeros((PLANE * 16, LANES), jnp.float32)
-
     def send_near(src, dst, phase):
         for dr, dc in NEIGHBOURS:
             remote(src, dst.at[(1 - dr) * 3 + (1 - dc)], phase, to(dr, dc))
@@ -360,9 +363,9 @@
                 (dr - 1) * CX, (brick - 3 * dr - 1) * CY, (lax.rem(tile - t + TILES + 1, TILES) - 1) * (KZ // TILES)
             )
             dx, dy, dz = (
-                (near0[brick, c, pl.ds(tile, 1), :] + shift[c].astype(jnp.float32)) - own[t, c] for c in range(3)
+                (nears[brick, c, pl.ds(tile, 1), :] + shift[c].astype(jnp.float32)) - own[t, c] for c in range(3)
             )
-            strength = own[t, 3] * near0[brick, 3, pl.ds(tile, 1), :]
+            strength = own[t, 3] * nears[brick, 3, pl.ds(tile, 1), :]
             sq = dx * dx + dy * dy + dz * dz
             inv = jnp.where(line + k * TILE == lane, 0.0, lax.rsqrt(sq))
             rho = sq * inv
@@ -387,11 +390,11 @@
             coef[at, 4] = ay * dz
             coef[at, 5] = az * dz - s1
 
-    def pairs(near, first_row):
+    def pairs(near, begin, end):
         block = 32
         blocks = TILE // block
 
-        @pl.loop(0, TILES * blocks)
+        @pl.loop(begin, end)
         def _(unit):
             t = unit // blocks
             cut = pl.ds(pl.multiple_of((unit - t * blocks) * block, block), block)
@@ -401,7 +404,7 @@
                 xx, xy, xz, yy, yz, zz = (coef[t * NBR + k, c, cut, :] for c in range(6))
                 out = []
                 for s in range(2):
-                    vx, vy, vz = (near[brick, first_row + 2 * c + s, pl.ds(tile, 1), :] for c in range(3))
+                    vx, vy, vz = (near[brick, 2 * c + s, pl.ds(tile, 1), :] for c in range(3))
                     out.append(sums[3 * s] + (xx * vx + xy * vy + xz * vz))
                     out.append(sums[3 * s + 1] + (xy * vx + yy * vy + yz * vz))
                     out.append(sums[3 * s + 2] + (xz * vx + yz * vy + zz * vz))
@@ -478,22 +481,22 @@
         tiles = swap_blocks(tiles)
         for slot in range(SLOTS):
             part = tiles[slot % 8][slot // 8 * PLANE : slot // 8 * PLANE + PLANE]
-            asend[op, pl.ds(SLOT_ROW[slot], PLANE, stride=16), :] = part
+            asend[op, pl.ds(slot, PLANE, stride=16), :] = part
 
     def send_planes(op):
         phase = 5 * op
-        mine = arecv.at[op, pl.ds(me_a * 16, 16)]
-        each_plane(lambda a, device: remote(asend.at[op, pl.ds(a * 16, 16)], mine, phase + 1, device))
-        keep(asend.at[op, pl.ds(me_a * 16, 16)], mine, phase + 1)
+        mine = arecv.at[op, pl.ds(me_a * 16, BRICK_ROWS)]
+        each_plane(lambda a, device: remote(asend.at[op, pl.ds(a * 16, BRICK_ROWS)], mine, phase + 1, device))
+        keep(asend.at[op, pl.ds(me_a * 16, BRICK_ROWS)], mine, phase + 1)
 
     row8 = lax.broadcasted_iota(jnp.int32, (8, LANES), 0)
 
     def gather_planes(op):
         phase = 5 * op
-        arrived(arecv.at[op], phase + 1)
+        arrived(arecv.at[op, pl.ds(0, PLANE * BRICK_ROWS)], phase + 1)
 
         def got(yb, x, one_core, yh):
-            at = (yb * 8 + x * 2 + one_core) * 16 + yh * 8
+            at = (yb * 8 + x * 2 + one_core) * 16 + yh * 6
             return arecv[op, at : at + 8, :]
 
         def joined(low, high):
@@ -509,22 +512,23 @@
                     low, high = low + got(yb, g - 1, 0, 1), high + got(yb, g - 1, 1, 1)
                 tile0, tile1 = joined(low, high)
                 edge = last0 if g == 1 else pltpu.roll(last0, (2 - 2 * g) % 8, 0)
-                rest = pltpu.roll(last1, 4, 0) if g == 0 else 0.0
+                rest = pltpu.roll(last1, 4 - g, 0) if g < 2 else 0.0
                 tile1 = jnp.where(
-                    row8 < 2, tile1, jnp.where(row8 < 4, edge, jnp.where(row8 < 6, rest, 0.0))
+                    row8 < 2, tile1, jnp.where(row8 < 4, edge, jnp.where(row8 == 4, rest, 0.0))
                 )
                 tiles.append(jnp.concatenate([tile0, tile1], axis=0))
         tiles = swap_blocks(tiles)
         for n in range(LINE):
-            bsend[op, n] = tiles[n]
-        each_line(lambda z, device: remote(bsend.at[op, z], brecv.at[op, me_z], phase + 2, device))
-        keep(bsend.at[op, me_z], brecv.at[op, me_z], phase + 2)
+            bsend[op, 16 * n : 16 * n + 16, :] = tiles[n]
+        mine = brecv.at[op, pl.ds(me_z * 16, LINE_ROWS)]
+        each_line(lambda z, device: remote(bsend.at[op, pl.ds(z * 16, LINE_ROWS)], mine, phase + 2, device))
+        keep(bsend.at[op, pl.ds(me_z * 16, LINE_ROWS)], mine, phase + 2)
 
     def convolve(op):
         phase = 5 * op
-        arrived(brecv.at[op], phase + 2)
+        arrived(brecv.at[op, pl.ds(0, LINE * LINE_ROWS)], phase + 2)
         lines = jnp.concatenate(
-            [brecv[op, 0:8].reshape(GX, LANES), brecv[op, 8:16].reshape(GX, LANES)], axis=1
+            [brecv[op, 0:GX, :], brecv[op, GX:, :]], axis=1
         )
         lines = halves(lines)
         part = [mm((hx[0, n], hx[1, n]), lines) for n in range(10)]
@@ -544,15 +548,16 @@
         for g in range(4):
             piece = jnp.where(x_bit, back_x(2 + g, edge), back_x(6 + g, edge))
             out = out + jnp.where(group == g, piece, 0.0)
-        csend[op, 0:8] = out[:, 0:LANES].reshape(8, 16, LANES)
-        csend[op, 8:16] = out[:, LANES:].reshape(8, 16, LANES)
-        each_line(lambda z, device: remote(csend.at[op, z], crecv.at[op, me_z], phase + 3, device))
-        keep(csend.at[op, me_z], crecv.at[op, me_z], phase + 3)
+        csend[op, 0:GX, :] = out[:, 0:LANES]
+        csend[op, GX:, :] = out[:, LANES:]
+        mine = crecv.at[op, pl.ds(me_z * 16, LINE_ROWS)]
+        each_line(lambda z, device: remote(csend.at[op, pl.ds(z * 16, LINE_ROWS)], mine, phase + 3, device))
+        keep(csend.at[op, pl.ds(me_z * 16, LINE_ROWS)], mine, phase + 3)
 
     def scatter_planes(op):
         phase = 5 * op
-        arrived(crecv.at[op], phase + 3)
-        tiles = swap_blocks([crecv[op, n] for n in range(LINE)])
+        arrived(crecv.at[op, pl.ds(0, LINE * LINE_ROWS)], phase + 3)
+        tiles = swap_blocks([crecv[op, 16 * n : 16 * n + 16, :] for n in range(LINE)])
         for yb in range(4):
             ends = [(tiles[4 * yb + g][0:8], tiles[4 * yb + g][8:16]) for g in range(4)]
             edges = [
@@ -561,26 +566,26 @@
             last0 = jnp.where(
                 row8 < 2, edges[0], jnp.where(row8 < 4, edges[1], jnp.where(row8 < 6, edges[2], edges[3]))
             )
-            ends.append((last0, pltpu.roll(ends[0][1], 4, 0)))
+            ends.append((last0, jnp.where(row8 == 0, pltpu.roll(ends[0][1], 4, 0), pltpu.roll(ends[1][1], 5, 0))))
             for n, (one, two) in enumerate(ends):
                 high = jnp.where(row8 < 4, pltpu.roll(one, 4, 0), pltpu.roll(two, 4, 0))
                 for x, yh in ((n, 0), (n - 1, 1)):
                     if 0 <= x < 4:
-                        at = (yb * 8 + x * 2) * 16 + yh * 8
+                        at = (yb * 8 + x * 2) * 16 + yh * 6
                         esend[op, at : at + 8, :] = one
                         esend[op, at + 16 : at + 24, :] = high
-        mine = erecv.at[op, pl.ds(me_a * 16, 16)]
-        each_plane(lambda a, device: remote(esend.at[op, pl.ds(a * 16, 16)], mine, phase + 4, device))
-        keep(esend.at[op, pl.ds(me_a * 16, 16)], mine, phase + 4)
+        mine = erecv.at[op, pl.ds(me_a * 16, BRICK_ROWS)]
+        each_plane(lambda a, device: remote(esend.at[op, pl.ds(a * 16, BRICK_ROWS)], mine, phase + 4, device))
+        keep(esend.at[op, pl.ds(me_a * 16, BRICK_ROWS)], mine, phase + 4)
 
     def sample(op):
         phase = 5 * op
-        arrived(erecv.at[op], phase + 4)
+        arrived(erecv.at[op, pl.ds(0, PLANE * BRICK_ROWS)], phase + 4)
         none = jnp.zeros((PLANE, LANES), jnp.float32)
         tiles = []
         for slot in range(8):
-            one = erecv[op, pl.ds(SLOT_ROW[slot], PLANE, stride=16), :]
-            two = erecv[op, pl.ds(SLOT_ROW[slot + 8], PLANE, stride=16), :] if slot < 4 else none
+            one = erecv[op, pl.ds(slot, PLANE, stride=16), :]
+            two = erecv[op, pl.ds(slot + 8, PLANE, stride=16), :] if slot < 4 else none
             tiles.append(jnp.concatenate([one, two], axis=0))
         tiles = swap_blocks(tiles)
         waves = jnp.concatenate(
@@ -604,15 +609,18 @@
 
     spread(0, d1)
     pl.semaphore_wait(barrier, PLANE - 1 + LINE - 1 + 8)
+    send_near(dstat, nears, 14)
     send_planes(0)
     send_near(dsend0, near0, 0)
     gather_planes(0)
-    arrived(near0, 0)
+    arrived(nears, 14)
     coefficients()
     for load in loads[2:]:
         load.wait()
+    arrived(near0, 0)
+    pairs(near0, 0, PAIRS_AHEAD[0])
     convolve(0)
-    pairs(near0, 4)
+    pairs(near0, PAIRS_AHEAD[0], PAIR_UNITS)
     finish_pairs()
     scatter_planes(0)
     recip = sample(0)
@@ -634,9 +642,10 @@
     gather_planes(1)
     sum_lines(0)
     arrived(near1, 5)
-    pairs(near1, 0)
+    pairs(near1, 0, PAIRS_AHEAD[1])
+    convolve(1)
+    pairs(near1, PAIRS_AHEAD[1], PAIR_UNITS)
     finish_pairs()
-    convolve(1)
     line = sum_done(0)
     progress = [unpack(line, s) for s in range(2)]
     step = [progress[s] / unpack(line, 2 + s) for s in range(2)]
@@ -670,13 +679,14 @@
         out_x[0, 0, d] = x2[2 * d : 2 * d + 2]
         out_r[0, 0, d] = r2[2 * d : 2 * d + 2]
 
+    left(nears.at[pl.ds(0, 8)], 14)
     left(near0.at[pl.ds(0, 8)], 0)
     left(near1.at[pl.ds(0, 8)], 5)
     for op in range(2):
-        left(arecv.at[op, pl.ds(0, (PLANE - 1) * 16)], 5 * op + 1)
-        left(brecv.at[op, pl.ds(0, LINE - 1)], 5 * op + 2)
-        left(crecv.at[op, pl.ds(0, LINE - 1)], 5 * op + 3)
-        left(erecv.at[op, pl.ds(0, (PLANE - 1) * 16)], 5 * op + 4)
+        left(arecv.at[op, pl.ds(0, (PLANE - 1) * BRICK_ROWS)], 5 * op + 1)
+        left(brecv.at[op, pl.ds(0, (LINE - 1) * LINE_ROWS)], 5 * op + 2)
+        left(crecv.at[op, pl.ds(0, (LINE - 1) * LINE_ROWS)], 5 * op + 3)
+        left(erecv.at[op, pl.ds(0, (PLANE - 1) * BRICK_ROWS)], 5 * op + 4)
         left(pplane.at[op, pl.ds(0, PLANE - 1)], 10 + 2 * op)
         left(pline.at[op, pl.ds(0, LINE - 1)], 11 + 2 * op)
 
@@ -707,12 +717,13 @@
             half(2, KZ, 2 * ATOMS), half(2, 2 * ATOMS, KZ), half(TILES * 6 * TILE, LANES), buf(GX, LANES),
             buf(TILES, 4, TILE, TILE), buf(TILES * NBR, 6, TILE, TILE), buf(TILES, 6, TILE, TILE),
             buf(8, ATOMS), buf(8, ATOMS), buf(3, 8, ATOMS), buf(2, GX, GY),
-            buf(10, TILES, TILE), buf(6, TILES, TILE), buf(9, 10, TILES, TILE), buf(9, 6, TILES, TILE),
+            buf(4, TILES, TILE), buf(6, TILES, TILE), buf(6, TILES, TILE),
+            buf(9, 4, TILES, TILE), buf(9, 6, TILES, TILE), buf(9, 6, TILES, TILE),
             buf(2, PLANE * 16, LANES), buf(2, PLANE * 16, LANES),
-            buf(2, LINE, 16, LANES), buf(2, LINE, 16, LANES), buf(2, LINE, 16, LANES), buf(2, LINE, 16, LANES),
+            buf(2, LINE * 16, LANES), buf(2, LINE * 16, LANES), buf(2, LINE * 16, LANES), buf(2, LINE * 16, LANES),
             buf(2, PLANE * 16, LANES), buf(2, PLANE * 16, LANES),
             buf(2, 1, LANES), buf(2, PLANE, 1, LANES), buf(2, 1, LANES), buf(2, LINE, 1, LANES),
-            pltpu.SemaphoreType.DMA((14,)), pltpu.SemaphoreType.DMA((14,)), pltpu.SemaphoreType.DMA((6,)),
+            pltpu.SemaphoreType.DMA((15,)), pltpu.SemaphoreType.DMA((15,)), pltpu.SemaphoreType.DMA((6,)),
         ],
         compiler_params=pltpu.CompilerParams(
             collective_id=0, has_side_effects=True, vmem_limit_bytes=56 * 1024 * 1024

time: 98.6 us -> 93.8 us (0.951)
  Pallas kernels: 95.8 us -> 91 us
    pallas_call x1, Pallas kernels: 95.8 us -> 91 us  [local(): pl.pallas_call(kernel, out_shape=(out, out), in_specs=[vmem] * 4 + [smem]...]
where the time goes in v5:
time: 93.8 us; the launch traced here: 93.6 us
  Pallas kernels  91 us (97%)
  local copies, waits for them, and re-layouts  1.92 us (2%)
    pallas_call x1, Pallas kernels, local(): pl.pallas_call(kernel, out_shape=(out, out), in_specs=[vmem] * 4 + [smem]...  91 us
    unnamed x4, local copies, waits for them, and re-layouts  1.92 us

profile of v5, /device:TPU:1, one launch (start us, length us, event | category | flops | bytes accessed | tf_op | source)
XLA Modules:
  0.0 93.6 jit_solution(13173948733715247100)
XLA Ops:
  0.6 91.0 %shard_map.149 = (f32[1,1,3,2,512]{4,3,2,1,0:T(2,128)}, f32[1,1,3,2,512]{4,3,2,1,0:T(2,128)}) custom-call(f32[1,1,3,2,512]{4,3,2,1,0:T(2,128)} %bitcast.6, f32[1,3,1,512]{3,2,1,0:T(1,128)} %bitcast.9, f32[1,1,1,512]{3,2,1,0:T(1,128)} %bitcast.11, s32[1,3,1,512]{3,2,1,0:T(1,128)} %bitcast.10, s32[1,1,4,12]{3,2,1,0:T(4,128)} %lists.1, ...), custom_call_target="tpu_custom_call" | custom-call | tf_op jit(solution)/shard_map/pallas_call | solution.py:708
  91.6 0.0 copy-start
  91.6 1.3 %copy.18 = f32[1,1,2,3,512]{4,2,3,1,0:T(2,128)} copy(f32[1,1,2,3,512]{4,2,3,1,0:T(2,128)} %bitcast.8) | data formatting | bytes 24576
  93.0 0.0 copy-done
  93.0 0.6 copy.19
Async XLA Ops:
  91.6 1.3 %copy-start = (f32[1,1,3,2,512]{4,3,2,1,0:T(2,128)S(1)}, f32[1,1,3,2,512]{4,3,2,1,0:T(2,128)}, u32[]{:S(2)}) copy-start(f32[1,1,3,2,512]{4,3,2,1,0:T(2,128)} %get-tuple-element.5) | copy-start | bytes 36868

commit v6 on v5

--- a/solution.py
+++ b/solution.py
@@ -61,7 +61,8 @@
 BRICK_ROWS = SLOTS
 LINE_ROWS = 13
 PAIR_UNITS = 16
-PAIRS_AHEAD = (4, 11)
+PAIRS_AHEAD = (12, 9)
+COEFS_AHEAD = 34
 
 
 def cas(rows, cols, length):
@@ -349,11 +350,11 @@
         entry = lists[0, 0, t, k]
         return entry // TILES, lax.rem(entry, TILES)
 
-    def coefficients():
+    def coefficients(begin, end):
         line = lax.broadcasted_iota(jnp.int32, (TILE, TILE), 0)
         lane = lax.broadcasted_iota(jnp.int32, (TILE, TILE), 1)
 
-        @pl.loop(0, TILES * NBR)
+        @pl.loop(begin, end)
         def _(at):
             t = at // NBR
             k = at - t * NBR
@@ -531,7 +532,7 @@
             [brecv[op, 0:GX, :], brecv[op, GX:, :]], axis=1
         )
         lines = halves(lines)
-        part = [mm((hx[0, n], hx[1, n]), lines) for n in range(10)]
+        part = mm((hx[0].reshape(10 * GX, LANES), hx[1].reshape(10 * GX, LANES)), lines).reshape(10, GX, 2 * LANES)
         body = jnp.where(x_bit, part[0], part[1])
         edge = jnp.where(x_bit, part[2], part[6])
         for g in range(1, 4):
@@ -541,13 +542,16 @@
         back = mm(halves(infl[...] * waves), (hy_t[0], hy_t[1]))
         body, edge = halves(back[:, 0 : 2 * LANES]), halves(back[:, 2 * LANES :])
 
-        def back_x(n, lines):
-            return mm((hx_t[0, n], hx_t[1, n]), lines)
-
-        out = jnp.where(x_bit, back_x(0, body), back_x(1, body))
+        def back_x(begin, end, lines):
+            count = end - begin
+            stack = tuple(hx_t[n, begin:end].reshape(count * GX, LANES) for n in range(2))
+            return mm(stack, lines).reshape(count, GX, 2 * LANES)
+
+        body = back_x(0, 2, body)
+        edge = back_x(2, 10, edge)
+        out = jnp.where(x_bit, body[0], body[1])
         for g in range(4):
-            piece = jnp.where(x_bit, back_x(2 + g, edge), back_x(6 + g, edge))
-            out = out + jnp.where(group == g, piece, 0.0)
+            out = out + jnp.where(group == g, jnp.where(x_bit, edge[g], edge[4 + g]), 0.0)
         csend[op, 0:GX, :] = out[:, 0:LANES]
         csend[op, GX:, :] = out[:, LANES:]
         mine = crecv.at[op, pl.ds(me_z * 16, LINE_ROWS)]
@@ -614,15 +618,16 @@
     send_near(dsend0, near0, 0)
     gather_planes(0)
     arrived(nears, 14)
-    coefficients()
+    coefficients(0, COEFS_AHEAD)
     for load in loads[2:]:
         load.wait()
+    convolve(0)
+    coefficients(COEFS_AHEAD, TILES * NBR)
     arrived(near0, 0)
     pairs(near0, 0, PAIRS_AHEAD[0])
-    convolve(0)
+    scatter_planes(0)
     pairs(near0, PAIRS_AHEAD[0], PAIR_UNITS)
     finish_pairs()
-    scatter_planes(0)
     recip = sample(0)
     direct1 = direct[...]
     q1 = near_part(d1) - direct1 + recip

time: 93.8 us -> 90.1 us (0.961)
  Pallas kernels: 91 us -> 87.3 us
    pallas_call x1, Pallas kernels: 91 us -> 87.3 us  [local(): pl.pallas_call(kernel, out_shape=(out, out), in_specs=[vmem] * 4 + [smem]...]
where the time goes in v6:
time: 90.1 us; the launch traced here: 89.9 us
  Pallas kernels  87.3 us (97%)
  local copies, waits for them, and re-layouts  1.92 us (2%)
    pallas_call x1, Pallas kernels, local(): pl.pallas_call(kernel, out_shape=(out, out), in_specs=[vmem] * 4 + [smem]...  87.3 us
    unnamed x4, local copies, waits for them, and re-layouts  1.92 us

profile of v6, /device:TPU:1, one launch (start us, length us, event | category | flops | bytes accessed | tf_op | source)
XLA Modules:
  0.0 89.9 jit_solution(8845073653708738882)
XLA Ops:
  0.6 87.3 %shard_map.149 = (f32[1,1,3,2,512]{4,3,2,1,0:T(2,128)}, f32[1,1,3,2,512]{4,3,2,1,0:T(2,128)}) custom-call(f32[1,1,3,2,512]{4,3,2,1,0:T(2,128)} %bitcast.6, f32[1,3,1,512]{3,2,1,0:T(1,128)} %bitcast.9, f32[1,1,1,512]{3,2,1,0:T(1,128)} %bitcast.11, s32[1,3,1,512]{3,2,1,0:T(1,128)} %bitcast.10, s32[1,1,4,12]{3,2,1,0:T(4,128)} %lists.1, ...), custom_call_target="tpu_custom_call" | custom-call | tf_op jit(solution)/shard_map/pallas_call | solution.py:713
  88.0 0.0 copy-start
  88.0 1.3 %copy.18 = f32[1,1,2,3,512]{4,2,3,1,0:T(2,128)} copy(f32[1,1,2,3,512]{4,2,3,1,0:T(2,128)} %bitcast.8) | data formatting | bytes 24576
  89.3 0.0 copy-done
  89.3 0.6 copy.19
Async XLA Ops:
  88.0 1.3 %copy-start = (f32[1,1,3,2,512]{4,3,2,1,0:T(2,128)S(1)}, f32[1,1,3,2,512]{4,3,2,1,0:T(2,128)}, u32[]{:S(2)}) copy-start(f32[1,1,3,2,512]{4,3,2,1,0:T(2,128)} %get-tuple-element.5) | copy-start | bytes 36868

commit v7 on v6

--- a/solution.py
+++ b/solution.py
@@ -61,8 +61,8 @@
 BRICK_ROWS = SLOTS
 LINE_ROWS = 13
 PAIR_UNITS = 16
-PAIRS_AHEAD = (12, 9)
-COEFS_AHEAD = 34
+PAIRS_AHEAD = (8, 12)
+COEFS_AHEAD = 26
 
 
 def cas(rows, cols, length):
@@ -670,12 +670,13 @@
     sum_lines(1)
     scatter_planes(1)
     w1 = keepv[2]
-    z1 = near_part(w1) - direct[...] + sample(1)
     q1 = keepv[1]
-    d2 = grown * d1 - step_w * w1
-    q2 = grown * q1 - step_w * z1
     x1 = step_w * d1
     r1 = r0 - step_w * q1
+    d2 = grown * d1 - step_w * w1
+    near_image = near_part(w1) - direct[...]
+    z1 = near_image + sample(1)
+    q2 = grown * q1 - step_w * z1
     line = sum_done(1)
     step2 = wide([following[s] / unpack(line, s) for s in range(2)])
     x2 = x1 + step2 * d2

time: 90.1 us -> 89.5 us (level)
  no operation moved by 1% of the time
where the time goes in v7:
time: 89.5 us; the launch traced here: 89.3 us
  Pallas kernels  86.7 us (97%)
  local copies, waits for them, and re-layouts  1.92 us (2%)
    pallas_call x1, Pallas kernels, local(): pl.pallas_call(kernel, out_shape=(out, out), in_specs=[vmem] * 4 + [smem]...  86.7 us
    unnamed x4, local copies, waits for them, and re-layouts  1.92 us

profile of v7, /device:TPU:1, one launch (start us, length us, event | category | flops | bytes accessed | tf_op | source)
XLA Modules:
  0.0 89.3 jit_solution(612834104007898418)
XLA Ops:
  0.6 86.7 %shard_map.149 = (f32[1,1,3,2,512]{4,3,2,1,0:T(2,128)}, f32[1,1,3,2,512]{4,3,2,1,0:T(2,128)}) custom-call(f32[1,1,3,2,512]{4,3,2,1,0:T(2,128)} %bitcast.6, f32[1,3,1,512]{3,2,1,0:T(1,128)} %bitcast.9, f32[1,1,1,512]{3,2,1,0:T(1,128)} %bitcast.11, s32[1,3,1,512]{3,2,1,0:T(1,128)} %bitcast.10, s32[1,1,4,12]{3,2,1,0:T(4,128)} %lists.1, ...), custom_call_target="tpu_custom_call" | custom-call | tf_op jit(solution)/shard_map/pallas_call | solution.py:714
  87.4 0.0 copy-start
  87.4 1.3 %copy.18 = f32[1,1,2,3,512]{4,2,3,1,0:T(2,128)} copy(f32[1,1,2,3,512]{4,2,3,1,0:T(2,128)} %bitcast.8) | data formatting | bytes 24576
  88.7 0.0 copy-done
  88.7 0.6 copy.19
Async XLA Ops:
  87.4 1.3 %copy-start = (f32[1,1,3,2,512]{4,3,2,1,0:T(2,128)S(1)}, f32[1,1,3,2,512]{4,3,2,1,0:T(2,128)}, u32[]{:S(2)}) copy-start(f32[1,1,3,2,512]{4,3,2,1,0:T(2,128)} %get-tuple-element.5) | copy-start | bytes 36868
